TPU v7x, 128 devices: a whole 4x4x4 slice. The times are simulated.
128 devices in a mesh: gx: 32 (over z, x, core), gy: 4 (over y).
Axes of the slice: x: 4, y: 4, z: 4, core: 2. Of those that a mesh axis runs over, the one named last changes fastest.
Arguments:
- node_feats: bfloat16 [32768, 6272], P(('gx', 'gy')), may hold values from -6 to 6
- halo_index: int32 [128, 4, 32], P(('gx', 'gy')), may hold values from 0 to 255
- edge_source: int32 [16384, 32], P(('gx', 'gy')), may hold values from 0 to 383, as said below
- edge_target: int32 [16384, 32], P(('gx', 'gy')), may hold values from 0 to 2
- edge_length: bfloat16 [16384, 32], P(('gx', 'gy')), may hold values from 0.796875 to 5.5
- edge_harmonics: bfloat16 [16384, 32, 49], P(('gx', 'gy')), may hold values from -4 to 4
- block_peer: int32 [128, 32], P(('gx', 'gy')), may hold values from 0 to 32, as said below
- radial_in: bfloat16 [128, 600], replicated, may hold values from -2 to 2
- radial_out: bfloat16 [600, 896], replicated, may hold values from -0.25 to 0.25
- mix_weight: bfloat16 [7, 128, 128], replicated, may hold values from -0.5 to 0.5
- harmonic_weight: bfloat16 [128, 128], replicated, may hold values from -0.5 to 0.5
- update_weight: bfloat16 [7, 128, 128], replicated, may hold values from -0.25 to 0.25
- norm_gain: float32 [7, 128], replicated, may hold values from 0.1 to 1.9
Outputs:
- updated: bfloat16 [32768, 6272], P(('gx', 'gy'))
Inputs may be any that keep to these rules, and one draw needn't show every extreme that they name: `block_peer`: in each row the entries below 32 are distinct. In every gy column some gx index is named by every device of that column. `edge_target`: 2 marks an empty edge slot. `edge_source`: the edges of each block have exactly 16 distinct sources.
All inputs are finite; a program needn't handle non-finite values.
Results may differ from a plain program's by a relative error of at most 0.0053.
Values may be sent and summed in bfloat16 or wider, within the bound.
A program may use at most 128 MiB of HBM per device.

v0:
```python
import jax
import jax.numpy as jnp
import numpy as np
from jax import lax
from jax.sharding import PartitionSpec as P

LMAX = 6
COEF = 49
C = 128
RB = 128
FEAT = 6272
EB = 32
TB = 2
KEEP = 96


cutoff_radius = 6.0
group_size = 8
norm_eps = 1e-06


def from_behind(block, axis, distance):
    devices = range(lax.axis_size(axis))
    route = [((i - distance) % len(devices), i) for i in devices]
    return lax.ppermute(block, axis, route)


def degree_index():
    return np.repeat(np.arange(LMAX + 1), 2 * np.arange(LMAX + 1) + 1)


def radial_features(distance):
    centers = cutoff_radius * (jnp.arange(RB, dtype=jnp.float32) + 0.5) / RB
    spread = 2.0 * cutoff_radius / RB
    envelope = 0.5 * (jnp.cos(jnp.pi * distance / cutoff_radius) + 1.0)
    offsets = (distance[:, None] - centers[None, :]) / spread
    return (jnp.exp(-0.5 * offsets * offsets) * envelope[:, None]).astype(jnp.bfloat16)


def edge_messages(
    sources_feat, distance, harmonics, radial_in, radial_out, mix_rows, harmonic_weight
):
    basis_vals = radial_features(distance.astype(jnp.float32))
    hidden = jax.nn.silu(jnp.dot(basis_vals, radial_in, preferred_element_type=jnp.float32)).astype(
        jnp.bfloat16
    )
    gate_vals = jnp.dot(hidden, radial_out, preferred_element_type=jnp.float32).astype(jnp.bfloat16)
    gate_vals = gate_vals.reshape(-1, LMAX + 1, C)
    gate_rows = gate_vals[:, degree_index(), :]
    scaled = (sources_feat.astype(jnp.float32) * gate_rows.astype(jnp.float32)).astype(jnp.bfloat16)
    mixed_rows = jnp.einsum("erc,rcd->erd", scaled, mix_rows, preferred_element_type=jnp.float32)
    scalar = jnp.dot(sources_feat[:, 0, :], harmonic_weight, preferred_element_type=jnp.float32)
    return (mixed_rows + harmonics.astype(jnp.float32)[:, :, None] * scalar[:, None, :]).astype(
        jnp.bfloat16
    )


def target_codes(targets):
    return jnp.where(targets < TB, targets + 1, 0).astype(jnp.bfloat16)


def block_sums(messages, slot_codes):
    labels = (jnp.arange(TB, dtype=jnp.int32) + 1).astype(jnp.bfloat16)
    onehot = (slot_codes[:, None, :] == labels[None, :, None]).astype(jnp.bfloat16)
    return jnp.einsum("gte,gef->gtf", onehot, messages, preferred_element_type=jnp.float32).astype(
        jnp.bfloat16
    )


def node_update(node_rows, gathered, update_weight, norm_gain):
    update_rows = update_weight[degree_index()]
    mixed = jnp.einsum("nrc,rcd->nrd", gathered, update_rows, preferred_element_type=jnp.float32)
    combined = node_rows.astype(jnp.float32).reshape(-1, COEF, C) + mixed
    inverse_rms = lax.rsqrt(jnp.mean(combined * combined, axis=(1, 2), keepdims=True) + norm_eps)
    gain_rows = norm_gain[degree_index()]
    return (combined * inverse_rms * gain_rows[None]).astype(jnp.bfloat16).reshape(-1, FEAT)


def along_gx(rows, step):
    return from_behind(rows, "gx", step)


def along_gy(rows, step):
    return from_behind(rows, "gy", step)


def per_device(
    node_feats,
    halo_index,
    edge_source,
    edge_target,
    edge_length,
    edge_harmonics,
    block_peer,
    radial_in,
    radial_out,
    mix_weight,
    harmonic_weight,
    update_weight,
    norm_gain,
):
    peer_count = lax.axis_size("gx")
    mix_rows = mix_weight[degree_index()]
    outgoing = node_feats[halo_index[0]]
    source_table = jnp.concatenate(
        [
            node_feats,
            along_gx(outgoing[0], 1),
            along_gx(outgoing[1], -1),
            along_gy(outgoing[2], 1),
            along_gy(outgoing[3], -1),
        ],
        axis=0,
    )

    def message_of(sources_feat, distance, harmonics):
        return edge_messages(
            sources_feat.reshape(-1, COEF, C),
            distance.reshape(-1),
            harmonics.reshape(-1, COEF),
            radial_in,
            radial_out,
            mix_rows,
            harmonic_weight,
        ).reshape(group_size, EB, FEAT)

    def run_kept(inputs):
        sources, targets, distance, harmonics = inputs
        gathered = source_table[sources.reshape(-1)]
        return block_sums(message_of(gathered, distance, harmonics), target_codes(targets))

    kept_totals = lax.map(
        run_kept,
        (
            edge_source[:KEEP].reshape(-1, group_size, EB),
            edge_target[:KEEP].reshape(-1, group_size, EB),
            edge_length[:KEEP].reshape(-1, group_size, EB),
            edge_harmonics[:KEEP].reshape(-1, group_size, EB, COEF),
        ),
    )
    kept_totals = kept_totals.reshape(KEEP, TB, FEAT)
    peer_rows = block_peer[0]
    slot_ids = jnp.arange(peer_count, dtype=jnp.int32)
    matched = peer_rows[None, :] == slot_ids[:, None]
    picked = jnp.sum(jnp.where(matched, slot_ids[None, :], 0), axis=1)
    present = jnp.any(matched, axis=1)
    chosen = KEEP + picked
    send_harm = jnp.where(
        present[:, None, None], edge_harmonics[chosen], jnp.zeros_like(edge_harmonics[chosen])
    )
    send_length = jnp.where(
        present[:, None], edge_length[chosen], jnp.zeros_like(edge_length[chosen])
    )
    send_codes = jnp.where(
        present[:, None],
        target_codes(edge_target[chosen]),
        jnp.zeros((peer_count, EB), jnp.bfloat16),
    )
    send_feat = source_table[edge_source[chosen].reshape(-1)].reshape(peer_count, EB, FEAT)
    send_feat = jnp.where(present[:, None, None], send_feat, jnp.zeros_like(send_feat))
    arrived = (
        lax.all_to_all(send_feat, "gx", split_axis=0, concat_axis=0, tiled=True),
        lax.all_to_all(send_harm, "gx", split_axis=0, concat_axis=0, tiled=True),
        lax.all_to_all(send_length, "gx", split_axis=0, concat_axis=0, tiled=True),
        lax.all_to_all(send_codes, "gx", split_axis=0, concat_axis=0, tiled=True),
    )
    arrived_feat, arrived_harm, arrived_length, arrived_codes = arrived
    arrived_inputs = (
        arrived_feat.reshape(-1, group_size, EB, FEAT),
        arrived_harm.reshape(-1, group_size, EB, COEF),
        arrived_length.reshape(-1, group_size, EB),
        arrived_codes.reshape(-1, group_size, EB),
    )

    def run_arrived(inputs):
        feats, harmonics, distance, slot_codes = inputs
        return block_sums(message_of(feats, distance, harmonics), slot_codes)

    arrived_totals = lax.map(run_arrived, arrived_inputs).reshape(peer_count, TB, FEAT)
    returned = lax.all_to_all(arrived_totals, "gx", split_axis=0, concat_axis=0, tiled=True)
    slot_live = peer_rows < peer_count
    own_totals = returned[jnp.minimum(peer_rows, peer_count - 1)]
    own_totals = jnp.where(slot_live[:, None, None], own_totals, jnp.zeros_like(own_totals))
    gathered_sums = jnp.concatenate([kept_totals, own_totals], axis=0).reshape(-1, COEF, C)
    return node_update(node_feats, gathered_sums, update_weight, norm_gain)


def solution(mesh):
    in_specs = (
        P(("gx", "gy"), None),
        P(("gx", "gy"), None, None),
        P(("gx", "gy"), None),
        P(("gx", "gy"), None),
        P(("gx", "gy"), None),
        P(("gx", "gy"), None, None),
        P(("gx", "gy"), None),
        P(),
        P(),
        P(),
        P(),
        P(),
        P(),
    )
    out_specs = P(("gx", "gy"), None)
    return jax.shard_map(
        per_device, mesh=mesh, in_specs=in_specs, out_specs=out_specs, check_vma=False
    )
```

profile of v0, /device:TPU:0, one launch (start us, length us, event | category | flops | bytes accessed | tf_op | source)
XLA Modules:
  0.0 912.8 jit_solution(5269769386418115493)
XLA Ops:
  2.2 6.5 gather_fusion.4
  11.5 5.8 collective-permute-start.1
  47.7 7.4 all-to-all-start
  56.9 25.2 %gather_fusion.8 = bf16[1024,6272]{1,0:T(8,128)(2,1)} fusion(bf16[384,6272]{1,0:T(8,128)(2,1)} %constant_dynamic-update-slice_fusion, s32[1024]{0:T(1024)S(1)} %broadcast_clamp_fusion), kind=kCustom, calls=%fused_computation.8 | custom fusion | bytes 25694208 | tf_op jit(solution)/shard_map/gather | solution.py:159
  82.7 7.8 all-to-all-start.3
  90.6 10.1 %broadcast_select_fusion = bf16[32,32,6272]{2,1,0:T(8,128)(2,1)} fusion(bf16[32,32,6272]{2,1,0:T(8,128)(2,1)} %bitcast.171, pred[32]{0:T(512)(128)(4,1)} %fusion.74), kind=kLoop, calls=%fused_computation.96 | loop fusion | flops 6422528 | bytes 25690144 | tf_op jit(solution)/shard_map/jit(_where)/select_n | solution.py:160
  101.4 7.5 all-to-all-start.1
  124.3 148.9 %all-to-all-done.1 = bf16[32,32,6272]{2,1,0:T(8,128)(2,1)} async-done(((bf16[32,32,6272]{2,1,0:T(8,128)(2,1)}), bf16[32,32,6272]{2,1,0:T(8,128)(2,1)}, u32[]{:S(2)}, u32[]{:S(2)}) %all-to-all-start.1) | async-done | bytes 12845088 | tf_op jit(solution)/shard_map/all_to_all | solution.py:162
  273.2 111.4 %while.27 = (s32[]{:T(128)}, bf16[4,8,2,6272]{3,2,1,0:T(2,128)(2,1)}, bf16[4,8,32]{2,1,0:T(8,128)(2,1)S(1)}, bf16[4,8,32,6272]{3,2,1,0:T(8,128)(2,1)}, bf16[4,8,...) while((s32[]{:T(128)}, ...), condition=%wide.region_5.6_spmd.clone, body=%wide.region_4.5_spmd.sunk.clone.sunk | while | flops 752975872 | bytes 51069460 | solution.py:179
  389.2 498.5 %while.26 = (s32[]{:T(128)}, bf16[12,8,2,6272]{3,2,1,0:T(2,128)(2,1)}, s32[12,8,32]{2,1,0:T(8,128)}, s32[12,8,32]{2,1,0:T(8,128)S(1)}, bf16[384,6272]{1,0:T(8,12...) while((s32[]{:T(128)}, ...), condition=%wide.region_1.2_spmd.clone, body=%wide.region_0.1_spmd.sunk.clone.sunk | while | flops 752978688 | bytes 57373724 | solution.py:132
  395.2 10.2 %gather_fusion = bf16[256,6272]{1,0:T(8,128)(2,1)} fusion(bf16[384,6272]{1,0:T(8,128)(2,1)} %get-tuple-element.640, s32[1024]{0:T(1024)S(1)} %pad_clamp_fusion.10), kind=kCustom, calls=%fused_computation.clone.1 | custom fusion | bytes 6423552 | tf_op jit(solution)/shard_map/while/body/eval_jaxpr/gather | solution.py:129
  436.7 10.2 %gather_fusion = bf16[256,6272]{1,0:T(8,128)(2,1)} fusion(bf16[384,6272]{1,0:T(8,128)(2,1)} %get-tuple-element.640, s32[1024]{0:T(1024)S(1)} %pad_clamp_fusion.10), kind=kCustom, calls=%fused_computation.clone.1 | custom fusion | bytes 6423552 | tf_op jit(solution)/shard_map/while/body/eval_jaxpr/gather | solution.py:129
  478.2 10.2 %gather_fusion = bf16[256,6272]{1,0:T(8,128)(2,1)} fusion(bf16[384,6272]{1,0:T(8,128)(2,1)} %get-tuple-element.640, s32[1024]{0:T(1024)S(1)} %pad_clamp_fusion.10), kind=kCustom, calls=%fused_computation.clone.1 | custom fusion | bytes 6423552 | tf_op jit(solution)/shard_map/while/body/eval_jaxpr/gather | solution.py:129
  519.7 10.2 %gather_fusion = bf16[256,6272]{1,0:T(8,128)(2,1)} fusion(bf16[384,6272]{1,0:T(8,128)(2,1)} %get-tuple-element.640, s32[1024]{0:T(1024)S(1)} %pad_clamp_fusion.10), kind=kCustom, calls=%fused_computation.clone.1 | custom fusion | bytes 6423552 | tf_op jit(solution)/shard_map/while/body/eval_jaxpr/gather | solution.py:129
  561.2 10.2 %gather_fusion = bf16[256,6272]{1,0:T(8,128)(2,1)} fusion(bf16[384,6272]{1,0:T(8,128)(2,1)} %get-tuple-element.640, s32[1024]{0:T(1024)S(1)} %pad_clamp_fusion.10), kind=kCustom, calls=%fused_computation.clone.1 | custom fusion | bytes 6423552 | tf_op jit(solution)/shard_map/while/body/eval_jaxpr/gather | solution.py:129
  602.7 10.2 %gather_fusion = bf16[256,6272]{1,0:T(8,128)(2,1)} fusion(bf16[384,6272]{1,0:T(8,128)(2,1)} %get-tuple-element.640, s32[1024]{0:T(1024)S(1)} %pad_clamp_fusion.10), kind=kCustom, calls=%fused_computation.clone.1 | custom fusion | bytes 6423552 | tf_op jit(solution)/shard_map/while/body/eval_jaxpr/gather | solution.py:129
  644.3 10.2 %gather_fusion = bf16[256,6272]{1,0:T(8,128)(2,1)} fusion(bf16[384,6272]{1,0:T(8,128)(2,1)} %get-tuple-element.640, s32[1024]{0:T(1024)S(1)} %pad_clamp_fusion.10), kind=kCustom, calls=%fused_computation.clone.1 | custom fusion | bytes 6423552 | tf_op jit(solution)/shard_map/while/body/eval_jaxpr/gather | solution.py:129
  685.8 10.2 %gather_fusion = bf16[256,6272]{1,0:T(8,128)(2,1)} fusion(bf16[384,6272]{1,0:T(8,128)(2,1)} %get-tuple-element.640, s32[1024]{0:T(1024)S(1)} %pad_clamp_fusion.10), kind=kCustom, calls=%fused_computation.clone.1 | custom fusion | bytes 6423552 | tf_op jit(solution)/shard_map/while/body/eval_jaxpr/gather | solution.py:129
  727.3 10.2 %gather_fusion = bf16[256,6272]{1,0:T(8,128)(2,1)} fusion(bf16[384,6272]{1,0:T(8,128)(2,1)} %get-tuple-element.640, s32[1024]{0:T(1024)S(1)} %pad_clamp_fusion.10), kind=kCustom, calls=%fused_computation.clone.1 | custom fusion | bytes 6423552 | tf_op jit(solution)/shard_map/while/body/eval_jaxpr/gather | solution.py:129
  768.8 10.2 %gather_fusion = bf16[256,6272]{1,0:T(8,128)(2,1)} fusion(bf16[384,6272]{1,0:T(8,128)(2,1)} %get-tuple-element.640, s32[1024]{0:T(1024)S(1)} %pad_clamp_fusion.10), kind=kCustom, calls=%fused_computation.clone.1 | custom fusion | bytes 6423552 | tf_op jit(solution)/shard_map/while/body/eval_jaxpr/gather | solution.py:129
  810.3 10.2 %gather_fusion = bf16[256,6272]{1,0:T(8,128)(2,1)} fusion(bf16[384,6272]{1,0:T(8,128)(2,1)} %get-tuple-element.640, s32[1024]{0:T(1024)S(1)} %pad_clamp_fusion.10), kind=kCustom, calls=%fused_computation.clone.1 | custom fusion | bytes 6423552 | tf_op jit(solution)/shard_map/while/body/eval_jaxpr/gather | solution.py:129
  851.8 10.2 %gather_fusion = bf16[256,6272]{1,0:T(8,128)(2,1)} fusion(bf16[384,6272]{1,0:T(8,128)(2,1)} %get-tuple-element.640, s32[1024]{0:T(1024)S(1)} %pad_clamp_fusion.10), kind=kCustom, calls=%fused_computation.clone.1 | custom fusion | bytes 6423552 | tf_op jit(solution)/shard_map/while/body/eval_jaxpr/gather | solution.py:129
  892.0 5.8 pad_maximum_fusion
  901.2 5.9 multiply_reduce_fusion
  (505 shorter events, 557.2 us)
Async XLA Ops:
  0.0 116.8 %copy-start = (bf16[7,128,128]{2,1,0:T(8,128)(2,1)S(1)}, bf16[7,128,128]{2,1,0:T(8,128)(2,1)}, u32[]{:S(2)}) copy-start(bf16[7,128,128]{2,1,0:T(8,128)(2,1)} %param.36) | copy-start | bytes 688132
  2.2 18.3 %copy-start.22 = (s32[1,32]{1,0:T(1,128)S(1)}, s32[1,32]{1,0:T(1,128)}, u32[]{:S(2)}) copy-start(s32[1,32]{1,0:T(1,128)} %param.33) | copy-start | bytes 388
  2.2 19.0 %copy-start.9 = (s32[128,32]{0,1:T(8,128)S(1)}, s32[128,32]{0,1:T(8,128)}, u32[]{:S(2)}) copy-start(s32[128,32]{0,1:T(8,128)} %param.30) | copy-start | bytes 49156
  8.7 12.5 %copy-start.18 = (bf16[128,32]{0,1:T(8,128)(2,1)S(1)}, bf16[128,32]{0,1:T(8,128)(2,1)}, u32[]{:S(2)}) copy-start(bf16[128,32]{0,1:T(8,128)(2,1)} %param.31) | copy-start | bytes 24580
  8.7 20.2 %copy-start.2 = (bf16[256,6272]{1,0:T(8,128)(2,1)S(1)}, bf16[256,6272]{1,0:T(8,128)(2,1)}, u32[]{:S(2)}) copy-start(bf16[256,6272]{1,0:T(8,128)(2,1)} %param.27) | copy-start | bytes 9633796
  11.5 30.8 %collective-permute-start = (bf16[32,6272]{1,0:T(8,128)(2,1)}, bf16[32,6272]{1,0:T(8,128)(2,1)}, u32[]{:S(2)}, u32[]{:S(2)}) collective-permute-start(bf16[32,6272]{1,0:T(8,128)(2,1)} %get-tuple-element.439), channel_id=1, source_target_pairs={{124,0},{0,4},{4,8},{8,12},{12,16},{16,20},{20,24},{24,28},{28,32}... | collective-permute-start | bytes 1204232 | tf_op jit(solution)/shard_map/ppermute | solution.py:25
  11.5 32.6 %collective-permute-start.1 = (bf16[32,6272]{1,0:T(8,128)(2,1)}, bf16[32,6272]{1,0:T(8,128)(2,1)}, u32[]{:S(2)}, u32[]{:S(2)}) collective-permute-start(bf16[32,6272]{1,0:T(8,128)(2,1)} %get-tuple-element.438), channel_id=1, source_target_pairs={{4,0},{8,4},{12,8},{16,12},{20,16},{24,20},{28,24},{32,28},{36,32}... | collective-permute-start | bytes 1204232 | tf_op jit(solution)/shard_map/ppermute | solution.py:25
  17.3 28.7 %collective-permute-start.2 = (bf16[32,6272]{1,0:T(8,128)(2,1)}, bf16[32,6272]{1,0:T(8,128)(2,1)}, u32[]{:S(2)}, u32[]{:S(2)}) collective-permute-start(bf16[32,6272]{1,0:T(8,128)(2,1)} %get-tuple-element.437), channel_id=1, source_target_pairs={{3,0},{0,1},{1,2},{2,3},{7,4},{4,5},{5,6},{6,7},{11,8},{8,9},{9,10... | collective-permute-start | bytes 1204232 | tf_op jit(solution)/shard_map/ppermute | solution.py:25
  18.9 36.3 %collective-permute-start.3 = (bf16[32,6272]{1,0:T(8,128)(2,1)}, bf16[32,6272]{1,0:T(8,128)(2,1)}, u32[]{:S(2)}, u32[]{:S(2)}) collective-permute-start(bf16[32,6272]{1,0:T(8,128)(2,1)} %get-tuple-element.436), channel_id=1, source_target_pairs={{1,0},{2,1},{3,2},{0,3},{5,4},{6,5},{7,6},{4,7},{9,8},{10,9},{11,1... | collective-permute-start | bytes 1204232 | tf_op jit(solution)/shard_map/ppermute | solution.py:25
  24.7 23.0 %all-to-all-start.2 = ((bf16[32,1,32]{2,1,0:T(2,128)(2,1)}), bf16[32,1,32]{2,1,0:T(2,128)(2,1)S(1)}, u32[]{:S(2)}, u32[]{:S(2)}) async-start(bf16[32,1,32]{2,1,0:T(2,128)(2,1)} %copy.129), calls=%async_computation.2 | async-start | bytes 32768 | tf_op jit(solution)/shard_map/all_to_all | solution.py:164
  29.0 9.6 %copy-start.20 = (pred[32]{0:T(512)(128)(4,1)S(1)}, pred[32]{0:T(512)(128)(4,1)}, u32[]{:S(2)}) copy-start(pred[32]{0:T(512)(128)(4,1)} %fusion.74) | copy-start | bytes 100
  47.7 34.4 %copy-start.13 = (bf16[32,1,32]{2,1,0:T(2,128)(2,1)}, bf16[32,1,32]{2,1,0:T(2,128)(2,1)S(1)}, u32[]{:S(2)}) copy-start(bf16[32,1,32]{2,1,0:T(2,128)(2,1)S(1)} %all-to-all-done.2) | copy-start | bytes 6148
  47.7 34.4 %all-to-all-start = ((bf16[32,1,32]{2,1,0:T(2,128)(2,1)}), bf16[32,1,32]{2,1,0:T(2,128)(2,1)S(1)}, u32[]{:S(2)}, u32[]{:S(2)}) async-start(bf16[32,1,32]{2,1,0:T(2,128)(2,1)} %copy.126), calls=%async_computation | async-start | bytes 32768 | tf_op jit(solution)/shard_map/all_to_all | solution.py:165
  82.7 18.0 %all-to-all-start.3 = ((bf16[32,2,784]{2,1,0:T(2,128)(2,1)}), bf16[32,2,784]{2,1,0:T(2,128)(2,1)S(1)}, u32[]{:S(2)}, u32[]{:S(2)}) async-start(bf16[32,2,784]{2,1,0:T(2,128)(2,1)} %reshape.629), calls=%async_computation.3 | async-start | bytes 229376 | tf_op jit(solution)/shard_map/all_to_all | solution.py:163
  101.4 171.8 %all-to-all-start.1 = ((bf16[32,32,6272]{2,1,0:T(8,128)(2,1)}), bf16[32,32,6272]{2,1,0:T(8,128)(2,1)}, u32[]{:S(2)}, u32[]{:S(2)}) async-start(bf16[32,32,6272]{2,1,0:T(8,128)(2,1)} %broadcast_select_fusion), calls=%async_computation.1 | async-start | bytes 25690112 | tf_op jit(solution)/shard_map/all_to_all | solution.py:162
  116.8 6.3 copy-start.14
  116.8 6.3 copy-start.16
  116.8 6.3 copy-start.7
  116.8 156.4 %copy-start.5 = (bf16[128,128]{1,0:T(8,128)(2,1)S(1)}, bf16[128,128]{1,0:T(8,128)(2,1)}, u32[]{:S(2)}) copy-start(bf16[128,128]{1,0:T(8,128)(2,1)} %param.37) | copy-start | bytes 98308
  384.6 503.1 %all-to-all-start.4 = ((bf16[32,2,6272]{2,1,0:T(2,128)(2,1)}), bf16[32,2,6272]{2,1,0:T(2,128)(2,1)}, u32[]{:S(2)}, u32[]{:S(2)}) async-start(bf16[32,2,6272]{2,1,0:T(2,128)(2,1)} %bitcast.178), calls=%async_computation.4 | async-start | bytes 1605632 | tf_op jit(solution)/shard_map/all_to_all | solution.py:180
  389.2 502.0 %copy-start.21 = (pred[32]{0:T(512)(128)(4,1)S(1)}, pred[32]{0:T(512)(128)(4,1)}, u32[]{:S(2)}) copy-start(pred[32]{0:T(512)(128)(4,1)} %broadcast_compare_fusion) | copy-start | bytes 100
  901.2 5.9 slice-start
  901.2 6.3 slice-start.1
  901.2 6.3 copy-start.8
  (11 other events, 37.4 us)
where the time goes:
time: 928 us; the launch traced here: 913 us
  local copies, waits for them, and re-layouts  541 us (58%)
  waiting for transfers between devices  149 us (16%)
  matrix products  145 us (16%)
  starting transfers between devices  40.5 us (4%)
  other arithmetic  34.8 us (4%)
    gather x24, local copies, waits for them, and re-layouts, run_kept(): gathered = source_table[sources.reshape(-1)]  177 us
    all_to_all x1, waiting for transfers between devices, per_device(): lax.all_to_all(send_feat, 'gx', split_axis=0, concat_axis=0, tiled=True)  149 us
    reshape x16, local copies, waits for them, and re-layouts, message_of(): return edge_messages(sources_feat.reshape(-1, COEF, C), distance.reshape(...  79.7 us
    dot_general x16, matrix products, edge_messages(): jnp.einsum('erc,rcd->erd', scaled, mix_rows, preferred_element_type=jnp.f...  70.5 us
    convert_element_type x16, local copies, waits for them, and re-layouts, edge_messages(): (mixed_rows + harmonics.astype(jnp.float32)[:, :, None] * scalar[:, None,...  62.5 us
    reshape x16, local copies, waits for them, and re-layouts, message_of(): sources_feat.reshape(-1, COEF, C)  58.3 us
    gather x16, local copies, waits for them, and re-layouts, edge_messages(): gate_rows = gate_vals[:, degree_index(), :]  43.6 us
    dot_general x16, matrix products, edge_messages(): jnp.dot(hidden, radial_out, preferred_element_type=jnp.float32)  37.6 us
  transfers between devices with their start and end apart: 9, of which 1 were waited for; matrix products, arithmetic and copies ran while one was open for 63% of the time, Pallas kernels for 0%

commit v1 on v0

v1 whole, which is shorter than its diff:
```python
import functools

import jax
import jax.numpy as jnp
import numpy as np
from jax import lax
from jax.experimental import pallas as pl
from jax.experimental.pallas import tpu as pltpu
from jax.sharding import PartitionSpec as P

LMAX = 6
DEG = 7
COEF = 49
C = 128
HID = 600
RB = 128
FEAT = 6272
EB = 32
TB = 2
KEEP = 96
BLOCKS = 128
NODES = 256
HALO = 32
TABLE = NODES + 4 * HALO
GROUP = 8
GROUPS = BLOCKS // GROUP
GE = GROUP * EB
GN = GROUP * TB
LENGTHS = 384
ROWS = 48
CHUNK = 4
CHUNKS = EB // CHUNK + 1
SLOTS = CHUNK * CHUNKS
ZERO_ROW = TABLE

cutoff_radius = 6.0
norm_eps = 1e-06

F32 = jnp.float32
BF16 = jnp.bfloat16
I32 = jnp.int32

DEGREE_OF = np.repeat(np.arange(LMAX + 1), 2 * np.arange(LMAX + 1) + 1)
TILES = ((1, 6), (2, 5), (3, 4))
PLACE = {}
for _tile, _pair in enumerate(TILES):
    _at = 16 * _tile
    for _degree in _pair:
        for _lm in range(_degree * _degree, (_degree + 1) * (_degree + 1)):
            PLACE[_lm] = _at
            _at += 1


def length_index(length):
    r = length.astype(F32)
    f = jnp.where(
        r < 1.0,
        (r - 0.796875) * 256.0,
        jnp.where(
            r < 2.0,
            (r - 1.0) * 128.0 + 52.0,
            jnp.where(r < 4.0, (r - 2.0) * 64.0 + 180.0, (r - 4.0) * 32.0 + 308.0),
        ),
    )
    return f.astype(I32)


def length_of(i):
    return jnp.where(
        i < 52.0,
        0.796875 + i / 256.0,
        jnp.where(
            i < 180.0,
            1.0 + (i - 52.0) / 128.0,
            jnp.where(i < 308.0, 2.0 + (i - 180.0) / 64.0, 4.0 + (i - 308.0) / 32.0),
        ),
    )


def outgoing_kernel(index_ref, nodes_ref, out_ref):
    row = lax.broadcasted_iota(I32, (4 * HALO, NODES), 1)
    onehot = (row == index_ref[...]).astype(F32).astype(BF16)
    for at in range(0, FEAT, 896):
        out_ref[:, at : at + 896] = jnp.dot(
            onehot, nodes_ref[:, at : at + 896], preferred_element_type=F32
        ).astype(BF16)


def fill_gates(radial_in_ref, radial_out_ref, gate_ref, gate0_ref, table_ref):
    i = lax.broadcasted_iota(I32, (LENGTHS, RB), 0).astype(F32)
    r = length_of(i)
    k = lax.broadcasted_iota(I32, (LENGTHS, RB), 1).astype(F32)
    centers = cutoff_radius * (k + 0.5) / RB
    spread = 2.0 * cutoff_radius / RB
    envelope = 0.5 * (jnp.cos(jnp.pi * r / cutoff_radius) + 1.0)
    offsets = (r - centers) / spread
    basis = (jnp.exp(-0.5 * offsets * offsets) * envelope).astype(BF16)
    hidden = jax.nn.silu(jnp.dot(basis, radial_in_ref[...], preferred_element_type=F32)).astype(BF16)
    gate = jnp.dot(hidden, radial_out_ref[...], preferred_element_type=F32).astype(BF16)
    gate0_ref[...] = gate[:, :C]
    gate_ref[...] = gate.astype(F32)
    row = lax.broadcasted_iota(I32, (16, C), 0)

    @pl.loop(0, LENGTHS // 8)
    def _(g):
        rows = [gate_ref[pl.ds(g * 8, 8), d * C : (d + 1) * C] for d in range(DEG)]
        for j in range(8):
            for tile, (low, high) in enumerate(TILES):
                first = jnp.broadcast_to(rows[low][j : j + 1], (16, C))
                second = jnp.broadcast_to(rows[high][j : j + 1], (16, C))
                table_ref[g * 8 + j, 16 * tile : 16 * tile + 16, :] = jnp.where(
                    row < 2 * low + 1, first, second
                ).astype(BF16)


def spread_rows(source_ref, count, base, wide_ref, table_ref):
    @pl.loop(0, count // 16)
    def _(g):
        at = pl.multiple_of(g * 16, 16)
        for lm in range(1, COEF):
            wide_ref[pl.ds(PLACE[lm], 16, stride=ROWS), :] = source_ref[
                pl.ds(at, 16), lm * C : (lm + 1) * C
            ].astype(F32)
        for j in range(16):
            table_ref[base + at + j] = wide_ref[j * ROWS : (j + 1) * ROWS, :].astype(BF16)


def fill_slots(payload_ref, target_ref, slot_ref):
    payload = payload_ref[...]
    target = target_ref[...]
    lower = (
        lax.broadcasted_iota(I32, (EB, EB), 0) > lax.broadcasted_iota(I32, (EB, EB), 1)
    ).astype(F32)
    zero = (target == 0).astype(F32)
    one = (target == 1).astype(F32)
    rank0 = jnp.dot(lower, zero, preferred_element_type=F32).astype(I32)
    rank1 = jnp.dot(lower, one, preferred_element_type=F32).astype(I32)
    slot = jnp.where(target == 0, rank0, jnp.where(target == 1, SLOTS - 1 - rank1, -1))
    nothing = ZERO_ROW * 512
    relative = payload - nothing
    for s in range(SLOTS):
        slot_ref[s : s + 1, :] = (
            jnp.sum(jnp.where(slot == s, relative, 0), axis=0, keepdims=True) + nothing
        )
    count0 = jnp.sum(zero, axis=0, keepdims=True).astype(I32)
    slot_ref[SLOTS : SLOTS + 1, :] = (count0 + (CHUNK - 1)) // CHUNK


def sum_edges(slots, table_ref, gates_ref, sums_ref):
    @pl.loop(0, BLOCKS)
    def _(b):
        first = slots[SLOTS, b]
        total0 = jnp.zeros((ROWS, C), F32)
        total1 = jnp.zeros((ROWS, C), F32)
        for j in range(CHUNKS):
            parts = []
            for k in range(CHUNK):
                p = slots[j * CHUNK + k, b]
                parts.append(
                    table_ref[lax.shift_right_logical(p, 9)] * gates_ref[lax.bitwise_and(p, 511)]
                )
            part = ((parts[0] + parts[1]) + (parts[2] + parts[3])).astype(F32)
            mine = j < first
            total0 = total0 + jnp.where(mine, part, 0.0)
            total1 = total1 + jnp.where(mine, 0.0, part)
        at = pl.multiple_of(b * (2 * ROWS), 8)
        sums_ref[pl.ds(at, ROWS), :] = total0
        sums_ref[pl.ds(at + ROWS, ROWS), :] = total1


def harmonic_sums(
    source_col_ref, length_col_ref, target_row_ref, harm_ref, scalars_ref, gate0_ref, harm_sums_ref, first_ref
):
    node = lax.broadcasted_iota(I32, (GN, GE), 0)
    edge = lax.broadcasted_iota(I32, (GN, GE), 1)
    same_block = lax.shift_right_logical(node, 1) == lax.shift_right_logical(edge, 5)
    wanted = jnp.where(same_block, lax.bitwise_and(node, 1), -1)
    row = lax.broadcasted_iota(I32, (GE, TABLE), 1)
    for g in range(GROUPS):
        pick = (source_col_ref[:, g : g + 1] == row).astype(F32).astype(BF16)
        scalars = jnp.dot(pick, scalars_ref[...], preferred_element_type=F32).astype(BF16)
        pick = (length_col_ref[:, g : g + 1] == row).astype(F32).astype(BF16)
        gates = jnp.dot(pick, gate0_ref[...], preferred_element_type=F32).astype(BF16)
        mask = (target_row_ref[g : g + 1, :] == wanted).astype(F32)
        first_ref[g * GN : (g + 1) * GN, :] = jnp.dot(
            mask.astype(BF16), scalars * gates, preferred_element_type=F32
        ).astype(BF16)
        harm = harm_ref[g].astype(F32)
        left = jnp.concatenate([(harm[lm : lm + 1, :] * mask).astype(BF16) for lm in range(COEF)], axis=0)
        right = jnp.dot(left, scalars, preferred_element_type=F32).astype(BF16)
        for lm in range(COEF):
            harm_sums_ref[lm, g * GN : (g + 1) * GN, :] = right[lm * GN : (lm + 1) * GN]


def update_nodes(
    nodes_ref, sums_ref, first_ref, harm_sums_ref, mix_ref, harmonic_ref, update_ref, gain_ref, combined_ref, out_ref
):
    squares = jnp.zeros((NODES, C), F32)
    for degree in range(DEG):
        update = update_ref[degree]
        both = jnp.concatenate([mix_ref[degree], harmonic_ref[...]], axis=0)
        weight = jnp.dot(both, update, preferred_element_type=F32).astype(BF16)
        for lm in range(degree * degree, (degree + 1) * (degree + 1)):
            if lm == 0:
                left = first_ref[...]
            else:
                left = sums_ref[pl.ds(PLACE[lm], NODES, stride=ROWS), :].astype(BF16)
            left = jnp.concatenate([left, harm_sums_ref[lm]], axis=1)
            mixed = jnp.dot(left, weight, preferred_element_type=F32)
            value = nodes_ref[:, lm * C : (lm + 1) * C].astype(F32) + mixed
            combined_ref[:, lm * C : (lm + 1) * C] = value
            squares = squares + value * value
    mean = jnp.sum(squares, axis=1, keepdims=True) / FEAT
    inverse = lax.rsqrt(mean + norm_eps)
    for lm in range(COEF):
        degree = int(DEGREE_OF[lm])
        out_ref[:, lm * C : (lm + 1) * C] = (
            combined_ref[:, lm * C : (lm + 1) * C] * inverse * gain_ref[degree : degree + 1, :]
        ).astype(BF16)


def layer_kernel(
    nodes_ref,
    halo0_ref,
    halo1_ref,
    halo2_ref,
    halo3_ref,
    payload_ref,
    target_ref,
    source_col_ref,
    length_col_ref,
    target_row_ref,
    harm_ref,
    radial_in_ref,
    radial_out_ref,
    mix_ref,
    harmonic_ref,
    update_ref,
    gain_ref,
    out_ref,
    gate_ref,
    gate0_ref,
    gates_ref,
    wide_ref,
    table_ref,
    scalars_ref,
    slot_ref,
    slots,
    sums_ref,
    first_ref,
    harm_sums_ref,
    combined_ref,
    slot_sem,
):
    fill_slots(payload_ref, target_ref, slot_ref)
    copy = pltpu.make_async_copy(slot_ref, slots, slot_sem)
    copy.start()
    fill_gates(radial_in_ref, radial_out_ref, gate_ref, gate0_ref, gates_ref)
    spread_rows(nodes_ref, NODES, 0, wide_ref, table_ref)
    scalars_ref[:NODES, :] = nodes_ref[:, :C]
    for k, halo_ref in enumerate((halo0_ref, halo1_ref, halo2_ref, halo3_ref)):
        base = NODES + HALO * k
        spread_rows(halo_ref, HALO, base, wide_ref, table_ref)
        scalars_ref[base : base + HALO, :] = halo_ref[:, :C]
    table_ref[ZERO_ROW] = jnp.zeros((ROWS, C), BF16)
    copy.wait()
    sum_edges(slots, table_ref, gates_ref, sums_ref)
    harmonic_sums(
        source_col_ref,
        length_col_ref,
        target_row_ref,
        harm_ref,
        scalars_ref,
        gate0_ref,
        harm_sums_ref,
        first_ref,
    )
    update_nodes(
        nodes_ref,
        sums_ref,
        first_ref,
        harm_sums_ref,
        mix_ref,
        harmonic_ref,
        update_ref,
        gain_ref,
        combined_ref,
        out_ref,
    )


def layer(*arrays):
    return pl.pallas_call(
        layer_kernel,
        out_shape=jax.ShapeDtypeStruct((NODES, FEAT), BF16),
        in_specs=[pl.BlockSpec(memory_space=pltpu.VMEM)] * len(arrays),
        out_specs=pl.BlockSpec(memory_space=pltpu.VMEM),
        scratch_shapes=[
            pltpu.VMEM((LENGTHS, DEG * C), F32),
            pltpu.VMEM((LENGTHS, C), BF16),
            pltpu.VMEM((LENGTHS, ROWS, C), BF16),
            pltpu.VMEM((16 * ROWS, C), F32),
            pltpu.VMEM((TABLE + 1, ROWS, C), BF16),
            pltpu.VMEM((TABLE, C), BF16),
            pltpu.VMEM((40, BLOCKS), I32),
            pltpu.SMEM((40, BLOCKS), I32),
            pltpu.VMEM((NODES * ROWS, C), F32),
            pltpu.VMEM((NODES, C), BF16),
            pltpu.VMEM((COEF, NODES, C), BF16),
            pltpu.VMEM((NODES, FEAT), F32),
            pltpu.SemaphoreType.DMA,
        ],
        compiler_params=pltpu.CompilerParams(vmem_limit_bytes=60 * 1024 * 1024),
        name="layer",
    )(*arrays)


def outgoing_rows(halo_index, node_feats):
    return pl.pallas_call(
        outgoing_kernel,
        out_shape=jax.ShapeDtypeStruct((4 * HALO, FEAT), BF16),
        in_specs=[pl.BlockSpec(memory_space=pltpu.VMEM)] * 2,
        out_specs=pl.BlockSpec(memory_space=pltpu.VMEM),
        compiler_params=pltpu.CompilerParams(vmem_limit_bytes=32 * 1024 * 1024),
        name="outgoing",
    )(halo_index.reshape(4 * HALO, 1), node_feats)


def edge_lists(edge_source, edge_target, edge_length, edge_harmonics, block_peer, peers):
    live = jnp.concatenate([jnp.ones((KEEP,), bool), block_peer[0] < peers])
    target = jnp.where(live[:, None], edge_target, TB)
    length = length_index(edge_length)
    payload = edge_source * 512 + length
    harm = edge_harmonics.reshape(GROUPS, GE, COEF).transpose(0, 2, 1)
    return (
        payload.T,
        target.T,
        edge_source.reshape(GROUPS, GE).T,
        length.reshape(GROUPS, GE).T,
        target.reshape(GROUPS, GE),
        harm,
    )


def shifted(rows, axis, step):
    size = lax.axis_size(axis)
    return lax.ppermute(rows, axis, [((i - step) % size, i) for i in range(size)])


def per_device(
    node_feats,
    halo_index,
    edge_source,
    edge_target,
    edge_length,
    edge_harmonics,
    block_peer,
    radial_in,
    radial_out,
    mix_weight,
    harmonic_weight,
    update_weight,
    norm_gain,
):
    outgoing = outgoing_rows(halo_index, node_feats)
    arrived = [
        shifted(outgoing[HALO * k : HALO * (k + 1)], axis, step)
        for k, (axis, step) in enumerate((("gx", 1), ("gx", -1), ("gy", 1), ("gy", -1)))
    ]
    lists = edge_lists(
        edge_source, edge_target, edge_length, edge_harmonics, block_peer, lax.axis_size("gx")
    )
    return layer(
        node_feats,
        *arrived,
        *lists,
        radial_in,
        radial_out,
        mix_weight,
        harmonic_weight,
        update_weight,
        norm_gain,
    )


def solution(mesh):
    split = ("gx", "gy")
    in_specs = (
        P(split, None),
        P(split, None, None),
        P(split, None),
        P(split, None),
        P(split, None),
        P(split, None, None),
        P(split, None),
        P(),
        P(),
        P(),
        P(),
        P(),
        P(),
    )
    return jax.shard_map(
        per_device, mesh=mesh, in_specs=in_specs, out_specs=P(split, None), check_vma=False
    )
```

time: 928 us -> 78.5 us (0.08); the launches traced: 913 us -> 78.4 us
  local copies, waits for them, and re-layouts: 541 us -> 10.6 us
  waiting for transfers between devices: 149 us -> 2.38 us
  matrix products: 145 us -> 0 us
  Pallas kernels: 0 us -> 55.4 us
  other arithmetic: 34.8 us -> 1.25 us
  starting transfers between devices: 40.5 us -> 8.49 us
    gather x50 -> x0, local copies, waits for them, and re-layouts: 266 us -> none  [the longest x24 177 us: run_kept(): gathered = source_table[sources.reshape(-1)]]
    reshape x64 -> x8, local copies, waits for them, and re-layouts: 155 us -> 5.12 us  [the longest x2 1.99 us: edge_lists(): harm = edge_harmonics.reshape(GROUPS, GE, COEF).transpose(0, 2, 1)]
    all_to_all x5 -> x0, waiting for transfers between devices: 149 us -> none  [the longest x1 149 us: per_device(): lax.all_to_all(send_feat, 'gx', split_axis=0, concat_axis=0, tiled=True)]
    dot_general x65 -> x0, matrix products: 145 us -> none  [the longest x16 70.5 us: edge_messages(): jnp.einsum('erc,rcd->erd', scaled, mix_rows, preferred_element_type=jnp.f...]
    convert_element_type x64 -> x1, local copies, waits for them, and re-layouts: 68.7 us -> 0.1 us  [length_index(): return f.astype(I32)]
    pallas_call x0 -> x2, Pallas kernels: none -> 55.4 us  [the longest x1 54.7 us: layer(): pl.pallas_call(layer_kernel, out_shape=jax.ShapeDtypeStruct((NODES, FEAT)...]
    all_to_all x5 -> x0, starting transfers between devices: 31.6 us -> none  [the longest x1 7.83 us: per_device(): lax.all_to_all(send_harm, 'gx', split_axis=0, concat_axis=0, tiled=True)]
    dynamic_slice x32 -> x0, local copies, waits for them, and re-layouts: 22 us -> none  [the longest x8 11.9 us: per_device(): lax.map(run_arrived, arrived_inputs).reshape(peer_count, TB, FEAT)]
  transfers between devices with their start and end apart: 9 -> 4, of which waited for: 1 -> 1; matrix products, arithmetic and copies ran while one was open for 63% -> 11% of each run, Pallas kernels for 0% -> 0%
where the time goes in v1:
time: 78.5 us; the launch traced here: 78.4 us
  Pallas kernels  55.4 us (71%)
  local copies, waits for them, and re-layouts  10.6 us (14%)
  starting transfers between devices  8.49 us (11%)
  waiting for transfers between devices  2.38 us (3%)
  other arithmetic  1.25 us (2%)
    pallas_call x1, Pallas kernels, layer(): pl.pallas_call(layer_kernel, out_shape=jax.ShapeDtypeStruct((NODES, FEAT)...  54.7 us
    ppermute x4, starting transfers between devices, shifted(): lax.ppermute(rows, axis, [((i - step) % size, i) for i in range(size)])  8.49 us
    unnamed x17, local copies, waits for them, and re-layouts  4.34 us
    ppermute x4, waiting for transfers between devices, shifted(): lax.ppermute(rows, axis, [((i - step) % size, i) for i in range(size)])  2.38 us
    reshape x2, local copies, waits for them, and re-layouts, edge_lists(): harm = edge_harmonics.reshape(GROUPS, GE, COEF).transpose(0, 2, 1)  1.99 us
  transfers between devices with their start and end apart: 4, of which 1 were waited for; matrix products, arithmetic and copies ran while one was open for 11% of the time, Pallas kernels for 0%

profile of v1, /device:TPU:0, one launch (start us, length us, event | category | flops | bytes accessed | tf_op | source)
XLA Modules:
  0.0 78.4 jit_solution(1401609650723548304)
XLA Ops:
  0.0 0.8 reshape.23.index_ref
  0.8 0.0 copy-start
  0.8 1.9 %copy-done = bf16[256,6272]{1,0:T(8,128)(2,1)S(1)} copy-done((bf16[256,6272]{1,0:T(8,128)(2,1)S(1)}, bf16[256,6272]{1,0:T(8,128)(2,1)}, u32[]{:S(2)}) %copy-start) | copy-done | bytes 3211288
  2.7 0.7 outgoing.1
  3.5 0.9 %fusion.11 = (bf16[32,6272]{1,0:T(8,128)(2,1)}, bf16[32,6272]{1,0:T(8,128)(2,1)S(1)}, bf16[32,6272]{1,0:T(8,128)(2,1)S(1)}, bf16[32,6272]{1,0:T(8,128)(2,1)S(1)}) fusion(bf16[128,6272]{1,0:T(8,128)(2,1)S(1)} %outgoing.1), kind=kLoop, calls=%fused_computation.22 | loop fusion | bytes 3211264 | tf_op jit(solution)/shard_map/slice | solution.py:367
  4.3 3.1 %collective-permute-start.3 = (bf16[32,6272]{1,0:T(8,128)(2,1)}, bf16[32,6272]{1,0:T(8,128)(2,1)}, u32[]{:S(2)}, u32[]{:S(2)}) collective-permute-start(bf16[32,6272]{1,0:T(8,128)(2,1)} %get-tuple-element.5), channel_id=1, source_target_pairs={{1,0},{2,1},{3,2},{0,3},{5,4},{6,5},{7,6},{4,7},{9,8},{10,9},{11,1... | collective-permute-start | bytes 1204232 | tf_op jit(solution)/shard_map/ppermute | solution.py:347
  7.4 5.4 %collective-permute-start.1 = (bf16[32,6272]{1,0:T(8,128)(2,1)S(1)}, bf16[32,6272]{1,0:T(8,128)(2,1)}, u32[]{:S(2)}, u32[]{:S(2)}) collective-permute-start(bf16[32,6272]{1,0:T(8,128)(2,1)S(1)} %get-tuple-element.7), channel_id=1, source_target_pairs={{4,0},{8,4},{12,8},{16,12},{20,16},{24,20},{28,24},{32,28},{36,32}... | collective-permute-start | bytes 1204232 | tf_op jit(solution)/shard_map/ppermute | solution.py:347
  12.9 0.1 copy.20
  13.0 0.1 reshape.20
  13.1 0.1 concatenate.3
  13.1 0.1 copy.22
  13.2 0.7 reshape.21.target_row_ref
  13.9 0.1 copy.18
  14.0 0.1 reshape.19
  14.1 0.7 copy.19
  14.9 0.7 copy.21
  15.6 0.8 %copy.25.radial_in_ref = bf16[128,600]{1,0:T(8,128)(2,1)} copy(bf16[128,600]{0,1:T(8,128)(2,1)S(1)} %copy-done.2) | data formatting | bytes 307200 | tf_op args[7]
  16.4 1.5 %copy.23 = bf16[128,32,49]{1,0,2:T(8,128)(2,1)S(1)} copy(bf16[128,32,49]{0,1,2:T(8,128)(2,1)S(1)} %copy-done.1) | data formatting | bytes 802816 | tf_op args[5]
  17.9 1.1 %reshape.22 = bf16[16,256,49]{1,0,2:T(8,128)(2,1)S(1)} reshape(bf16[128,32,49]{1,0,2:T(8,128)(2,1)S(1)} %copy.23) | data formatting | bytes 802816 | tf_op jit(solution)/shard_map/reshape | solution.py:334
  19.0 0.9 %copy.27 = bf16[16,256,49]{1,2,0:T(8,128)(2,1)} copy(bf16[16,256,49]{1,0,2:T(8,128)(2,1)S(1)} %reshape.22) | data formatting | bytes 802816 | tf_op jit(solution)/shard_map/reshape | solution.py:334
  19.9 0.6 fusion.12.target_ref
  20.5 0.6 add_bitcast_fusion.payload_ref
  21.2 2.4 %collective-permute-done.halo0_ref = bf16[32,6272]{1,0:T(8,128)(2,1)} collective-permute-done((bf16[32,6272]{1,0:T(8,128)(2,1)S(1)}, bf16[32,6272]{1,0:T(8,128)(2,1)}, u32[]{:S(2)}, u32[]{:S(2)}) %collective-permute-start) | collective-permute-done | bytes 401440 | tf_op jit(solution)/shard_map/ppermute | solution.py:347
  23.5 54.7 %layer.1 = bf16[256,6272]{1,0:T(8,128)(2,1)} custom-call(bf16[256,6272]{1,0:T(8,128)(2,1)} %nodes_ref.3, bf16[32,6272]{1,0:T(8,128)(2,1)} %collective-permute-done.halo0_ref, bf16[32,6272]{1,0:T(8,128)(2,1)} %collective-permute-done.1.halo1_ref, bf16[32,6272]{1,0:T(8,128)(2,1)} %collective-permute-done.2.halo2_ref, ...), custom_call_target="tpu_custom_call" | custom-call | tf_op jit(solution)/shard_map/layer/pallas_call | solution.py:293
  (20 shorter events, 0.1 us)
Async XLA Ops:
  0.8 1.9 %copy-start = (bf16[256,6272]{1,0:T(8,128)(2,1)S(1)}, bf16[256,6272]{1,0:T(8,128)(2,1)}, u32[]{:S(2)}) copy-start(bf16[256,6272]{1,0:T(8,128)(2,1)} %nodes_ref.3) | copy-start | bytes 9633796
  3.4 9.4 %copy-start.6 = (s32[1,32]{1,0:T(1,128)S(1)}, s32[1,32]{1,0:T(1,128)}, u32[]{:S(2)}) copy-start(s32[1,32]{1,0:T(1,128)} %param.19) | copy-start | bytes 388
  3.4 9.4 %copy-start.5 = (bf16[128,32]{0,1:T(8,128)(2,1)S(1)}, bf16[128,32]{0,1:T(8,128)(2,1)}, u32[]{:S(2)}) copy-start(bf16[128,32]{0,1:T(8,128)(2,1)} %param.17) | copy-start | bytes 24580
  3.4 9.7 %copy-start.4 = (s32[128,32]{0,1:T(8,128)S(1)}, s32[128,32]{0,1:T(8,128)}, u32[]{:S(2)}) copy-start(s32[128,32]{0,1:T(8,128)} %param.16) | copy-start | bytes 49156
  3.4 10.5 %copy-start.3 = (s32[128,32]{0,1:T(8,128)S(1)}, s32[128,32]{0,1:T(8,128)}, u32[]{:S(2)}) copy-start(s32[128,32]{0,1:T(8,128)} %param.15) | copy-start | bytes 49156
  3.4 12.2 %copy-start.2 = (bf16[128,600]{0,1:T(8,128)(2,1)S(1)}, bf16[128,600]{0,1:T(8,128)(2,1)}, u32[]{:S(2)}) copy-start(bf16[128,600]{0,1:T(8,128)(2,1)} %param.20) | copy-start | bytes 460804
  3.5 13.0 %copy-start.1 = (bf16[128,32,49]{0,1,2:T(8,128)(2,1)S(1)}, bf16[128,32,49]{0,1,2:T(8,128)(2,1)}, u32[]{:S(2)}) copy-start(bf16[128,32,49]{0,1,2:T(8,128)(2,1)} %param.18) | copy-start | bytes 1204228
  4.3 16.8 %collective-permute-start.3 = (bf16[32,6272]{1,0:T(8,128)(2,1)}, bf16[32,6272]{1,0:T(8,128)(2,1)}, u32[]{:S(2)}, u32[]{:S(2)}) collective-permute-start(bf16[32,6272]{1,0:T(8,128)(2,1)} %get-tuple-element.5), channel_id=1, source_target_pairs={{1,0},{2,1},{3,2},{0,3},{5,4},{6,5},{7,6},{4,7},{9,8},{10,9},{11,1... | collective-permute-start | bytes 1204232 | tf_op jit(solution)/shard_map/ppermute | solution.py:347
  7.4 13.7 %collective-permute-start.2 = (bf16[32,6272]{1,0:T(8,128)(2,1)S(1)}, bf16[32,6272]{1,0:T(8,128)(2,1)}, u32[]{:S(2)}, u32[]{:S(2)}) collective-permute-start(bf16[32,6272]{1,0:T(8,128)(2,1)S(1)} %get-tuple-element.6), channel_id=1, source_target_pairs={{3,0},{0,1},{1,2},{2,3},{7,4},{4,5},{5,6},{6,7},{11,8},{8,9},{9,10... | collective-permute-start | bytes 1204232 | tf_op jit(solution)/shard_map/ppermute | solution.py:347
  7.4 13.7 %collective-permute-start.1 = (bf16[32,6272]{1,0:T(8,128)(2,1)S(1)}, bf16[32,6272]{1,0:T(8,128)(2,1)}, u32[]{:S(2)}, u32[]{:S(2)}) collective-permute-start(bf16[32,6272]{1,0:T(8,128)(2,1)S(1)} %get-tuple-element.7), channel_id=1, source_target_pairs={{4,0},{8,4},{12,8},{16,12},{20,16},{24,20},{28,24},{32,28},{36,32}... | collective-permute-start | bytes 1204232 | tf_op jit(solution)/shard_map/ppermute | solution.py:347
  12.8 10.7 %collective-permute-start = (bf16[32,6272]{1,0:T(8,128)(2,1)S(1)}, bf16[32,6272]{1,0:T(8,128)(2,1)}, u32[]{:S(2)}, u32[]{:S(2)}) collective-permute-start(bf16[32,6272]{1,0:T(8,128)(2,1)S(1)} %get-tuple-element.8), channel_id=1, source_target_pairs={{124,0},{0,4},{4,8},{8,12},{12,16},{16,20},{20,24},{24,28},{28,32}... | collective-permute-start | bytes 1204232 | tf_op jit(solution)/shard_map/ppermute | solution.py:347

commit v2 on v1

v2 whole, which is shorter than its diff:
```python
import functools

import jax
import jax.numpy as jnp
import numpy as np
from jax import lax
from jax.experimental import pallas as pl
from jax.experimental.pallas import tpu as pltpu
from jax.sharding import PartitionSpec as P

LMAX = 6
DEG = 7
COEF = 49
C = 128
HID = 600
RB = 128
FEAT = 6272
EB = 32
TB = 2
KEEP = 96
BLOCKS = 128
NODES = 256
HALO = 32
TABLE = NODES + 4 * HALO
GROUP = 8
GROUPS = BLOCKS // GROUP
GE = GROUP * EB
GN = GROUP * TB
LENGTHS = 384
ROWS = 48
CHUNK = 4
CHUNKS = EB // CHUNK + 1
SLOTS = CHUNK * CHUNKS
ZERO_ROW = TABLE

cutoff_radius = 6.0
norm_eps = 1e-06

F32 = jnp.float32
BF16 = jnp.bfloat16
I32 = jnp.int32

DEGREE_OF = np.repeat(np.arange(LMAX + 1), 2 * np.arange(LMAX + 1) + 1)
PARTS = 3
WIDE = 2 * C
HALF = 64
PIECE = 7 * C
PIECES = FEAT // PIECE
MESH = pl.DeviceIdType.MESH


def length_index(length):
    r = length.astype(F32)
    f = jnp.where(
        r < 1.0,
        (r - 0.796875) * 256.0,
        jnp.where(
            r < 2.0,
            (r - 1.0) * 128.0 + 52.0,
            jnp.where(r < 4.0, (r - 2.0) * 64.0 + 180.0, (r - 4.0) * 32.0 + 308.0),
        ),
    )
    return f.astype(I32)


def length_of(i):
    return jnp.where(
        i < 52.0,
        0.796875 + i / 256.0,
        jnp.where(
            i < 180.0,
            1.0 + (i - 52.0) / 128.0,
            jnp.where(i < 308.0, 2.0 + (i - 180.0) / 64.0, 4.0 + (i - 308.0) / 32.0),
        ),
    )


def fill_gates(radial_in_ref, radial_out_ref, gate_ref, gate0_ref, table_ref):
    i = lax.broadcasted_iota(I32, (LENGTHS, RB), 0).astype(F32)
    r = length_of(i)
    k = lax.broadcasted_iota(I32, (LENGTHS, RB), 1).astype(F32)
    centers = cutoff_radius * (k + 0.5) / RB
    spread = 2.0 * cutoff_radius / RB
    envelope = 0.5 * (jnp.cos(jnp.pi * r / cutoff_radius) + 1.0)
    offsets = (r - centers) / spread
    basis = (jnp.exp(-0.5 * offsets * offsets) * envelope).astype(BF16)
    hidden = lax.dot_general(
        basis, radial_in_ref[...], (((1,), (1,)), ((), ())), preferred_element_type=F32
    )
    hidden = jax.nn.silu(hidden).astype(BF16)
    gate = jnp.dot(hidden, radial_out_ref[...], preferred_element_type=F32).astype(BF16)
    gate0_ref[...] = gate[:, :C]
    gate_ref[...] = gate.astype(F32)
    row = lax.broadcasted_iota(I32, (8, C), 0)

    @pl.loop(0, LENGTHS // 8)
    def _(g):
        rows = [gate_ref[pl.ds(g * 8, 8), d * C : (d + 1) * C] for d in range(DEG)]
        at = g * (8 * PARTS)
        for j in range(8):
            tiles = []
            for tile in range(6):
                first = int(DEGREE_OF[1 + 8 * tile])
                last = int(DEGREE_OF[8 + 8 * tile])
                value = jnp.broadcast_to(rows[first][j : j + 1], (8, C))
                if last != first:
                    split = last * last - (1 + 8 * tile)
                    value = jnp.where(
                        row < split, value, jnp.broadcast_to(rows[last][j : j + 1], (8, C))
                    )
                tiles.append(value)
            for i in range(3):
                table_ref[at + j * PARTS + i] = jnp.concatenate(
                    tiles[2 * i : 2 * i + 2], axis=1
                ).astype(BF16)


def spread_rows(source_ref, count, base, wide_ref, table_ref):
    @pl.loop(0, count // 16)
    def _(g):
        at = pl.multiple_of(g * 16, 16)
        for lm in range(1, COEF, 2):
            pair = source_ref[pl.ds(at, 16), lm * C : (lm + 2) * C].astype(F32)
            wide_ref[pl.ds(lm - 1, 16, stride=ROWS), :] = pair[:, :C]
            wide_ref[pl.ds(lm, 16, stride=ROWS), :] = pair[:, C:]
        to = (base + at) * PARTS
        for j in range(16):
            for i in range(3):
                low = j * ROWS + 16 * i
                table_ref[to + j * PARTS + i] = jnp.concatenate(
                    [wide_ref[low : low + 8, :], wide_ref[low + 8 : low + 16, :]], axis=1
                ).astype(BF16)


def column_of(row, size):
    diagonal = lax.broadcasted_iota(I32, (size, size), 0) == lax.broadcasted_iota(I32, (size, size), 1)
    return jnp.sum(jnp.where(diagonal, jnp.broadcast_to(row, (size, size)), 0), axis=1, keepdims=True)


def fill_lists(peer_ref, source_ref, target_ref, length_ref, peers, across_refs, slot_ref):
    peer = jnp.concatenate([jnp.zeros((1, KEEP), I32), peer_ref[...]], axis=1)
    target = jnp.where(peer < peers, target_ref[...], TB)
    source = source_ref[...]
    length = length_index(length_ref[...])
    for ref, value in zip(across_refs, (source, length, target)):
        ref[...] = value.T
    lower = (
        lax.broadcasted_iota(I32, (EB, EB), 0) > lax.broadcasted_iota(I32, (EB, EB), 1)
    ).astype(F32)
    zero = (target == 0).astype(F32)
    one = (target == 1).astype(F32)
    rank0 = jnp.dot(lower, zero, preferred_element_type=F32).astype(I32)
    rank1 = jnp.dot(lower, one, preferred_element_type=F32).astype(I32)
    slot = jnp.where(target == 0, rank0, jnp.where(target == 1, SLOTS - 1 - rank1, -1))
    relative = (source - ZERO_ROW) * PARTS
    length = length * PARTS
    count0 = jnp.sum(zero, axis=0, keepdims=True).astype(I32)
    rows = []
    for s in range(SLOTS):
        rows.append(jnp.sum(jnp.where(slot == s, relative, 0), axis=0, keepdims=True) + ZERO_ROW * PARTS)
    rows.append(lax.shift_right_logical(count0 + (CHUNK - 1), 2))
    rows.append(jnp.zeros((HALF - SLOTS - 1, BLOCKS), I32))
    for s in range(SLOTS):
        rows.append(jnp.sum(jnp.where(slot == s, length, 0), axis=0, keepdims=True))
    rows.append(jnp.zeros((HALF - SLOTS, BLOCKS), I32))
    slot_ref[...] = jnp.concatenate(rows, axis=0).T


def by_group(ref):
    return jnp.concatenate([ref[pl.ds(b, GROUPS, stride=GROUP), :] for b in range(GROUP)], axis=1)


def transposed(x):
    rows = x.shape[1]
    identity = (
        lax.broadcasted_iota(I32, (rows, rows), 0) == lax.broadcasted_iota(I32, (rows, rows), 1)
    ).astype(F32).astype(BF16)
    return lax.dot_general(identity, x, (((1,), (1,)), ((), ())), preferred_element_type=F32)


def harmonic_sums(
    across_refs, harm_ref, scalars_ref, gate0_ref, rows_ref, turned_ref, harm_rows_ref, harm_sums_ref, first_ref
):
    for n, ref in enumerate(across_refs):
        rows_ref[n] = by_group(ref)

    @pl.loop(0, COEF // 7)
    def _(step):
        for n in range(7):
            turned_ref[n] = harm_ref[step * 7 + n].astype(F32).T
            at = pl.multiple_of((step * 7 + n) * GROUPS, GROUPS)
            harm_rows_ref[pl.ds(at, GROUPS), :] = by_group(turned_ref.at[n])

    node = lax.broadcasted_iota(I32, (GN, GE), 0)
    edge = lax.broadcasted_iota(I32, (GN, GE), 1)
    same_block = lax.shift_right_logical(node, 1) == lax.shift_right_logical(edge, 5)
    wanted = jnp.where(same_block, lax.bitwise_and(node, 1), -1)
    across = (((1,), (1,)), ((), ()))
    scalars = transposed(scalars_ref[...]).astype(BF16)
    gate0 = transposed(gate0_ref[...]).astype(BF16)

    @pl.loop(0, GROUPS)
    def _(g):
        row = lax.broadcasted_iota(I32, (TABLE, GE), 0)
        pick = (rows_ref[0, pl.ds(g, 1), :] == row).astype(F32).astype(BF16)
        scalar = jnp.dot(scalars, pick, preferred_element_type=F32).astype(BF16)
        pick = (rows_ref[1, pl.ds(g, 1), :] == row).astype(F32).astype(BF16)
        gate = jnp.dot(gate0, pick, preferred_element_type=F32).astype(BF16)
        mask = (rows_ref[2, pl.ds(g, 1), :] == wanted).astype(F32)
        at = pl.multiple_of(g * GN, GN)
        first_ref[pl.ds(at, GN), :] = lax.dot_general(
            mask.astype(BF16), scalar * gate, across, preferred_element_type=F32
        )
        left = jnp.concatenate(
            [
                (harm_rows_ref[pl.ds(lm * GROUPS + g, 1), :] * mask).astype(BF16)
                for lm in range(COEF)
            ],
            axis=0,
        )
        right = lax.dot_general(left, scalar, across, preferred_element_type=F32)
        for lm in range(COEF):
            harm_sums_ref[lm, pl.ds(at, GN), :] = right[lm * GN : (lm + 1) * GN]


def gather_kernel(
    nodes_hbm,
    halo_hbm,
    peer_hbm,
    source_hbm,
    target_hbm,
    length_hbm,
    radial_in_hbm,
    radial_out_hbm,
    harm_hbm,
    table_ref,
    gates_ref,
    harm_sums_ref,
    first_ref,
    slot_ref,
    halo_ref,
    peer_ref,
    source_ref,
    target_ref,
    length_ref,
    radial_in_ref,
    harm_ref,
    nodes_ref,
    radial_out_ref,
    send_ref,
    arrived_ref,
    gate_ref,
    gate0_ref,
    wide_ref,
    scalars_ref,
    source_across_ref,
    length_across_ref,
    target_across_ref,
    rows_ref,
    turned_ref,
    harm_rows_ref,
    load_sem,
    other_sem,
    send_sem,
    recv_sem,
    peers,
    columns,
):
    p, q = lax.axis_index("gx"), lax.axis_index("gy")
    ahead, behind = lax.rem(p + 1, peers), lax.rem(p + peers - 1, peers)
    above, below = lax.rem(q + 1, columns), lax.rem(q + columns - 1, columns)
    neighbours = ((ahead, q), (behind, q), (p, above), (p, below))

    smalls = []
    for n, (source, target) in enumerate(
        (
            (halo_hbm, halo_ref),
            (peer_hbm, peer_ref),
            (source_hbm, source_ref),
            (target_hbm, target_ref),
            (length_hbm, length_ref),
            (radial_in_hbm, radial_in_ref),
            (radial_out_hbm, radial_out_ref),
            (harm_hbm, harm_ref),
        )
    ):
        smalls.append(pltpu.make_async_copy(source, target, other_sem.at[n]))
    smalls[0].start()
    loads = []
    for c in range(PIECES):
        cut = pl.ds(c * PIECE, PIECE)
        load = pltpu.make_async_copy(nodes_hbm.at[:, cut], nodes_ref.at[:, cut], load_sem.at[c])
        load.start()
        loads.append(load)
    for load in smalls[1:]:
        load.start()

    barrier = pltpu.get_barrier_semaphore()
    for neighbour in neighbours:
        pl.semaphore_signal(barrier, inc=1, device_id=neighbour, device_id_type=MESH)

    smalls[0].wait()
    index = column_of(jnp.concatenate([halo_ref[k : k + 1, :] for k in range(4)], axis=1), 4 * HALO)
    pick = (lax.broadcasted_iota(I32, (4 * HALO, NODES), 1) == index).astype(F32).astype(BF16)
    pl.semaphore_wait(barrier, 4)
    copies = []
    for c in range(PIECES):
        loads[c].wait()
        cut = pl.ds(c * PIECE, PIECE)
        send_ref[:, cut] = jnp.dot(pick, nodes_ref[:, cut], preferred_element_type=F32).astype(BF16)
        for k in (2, 3, 0, 1):
            part = pl.ds(k * HALO, HALO)
            copy = pltpu.make_async_remote_copy(
                src_ref=send_ref.at[part, cut],
                dst_ref=arrived_ref.at[part, cut],
                send_sem=send_sem.at[k, c],
                recv_sem=recv_sem.at[k, c],
                device_id=neighbours[k],
                device_id_type=MESH,
            )
            copy.start()
            copies.append(copy)

    for load in smalls[1:5]:
        load.wait()
    across_refs = (source_across_ref, length_across_ref, target_across_ref)
    fill_lists(peer_ref, source_ref, target_ref, length_ref, peers, across_refs, slot_ref)
    smalls[5].wait()
    smalls[6].wait()
    fill_gates(radial_in_ref, radial_out_ref, gate_ref, gate0_ref, gates_ref)
    spread_rows(nodes_ref, NODES, 0, wide_ref, table_ref)
    table_ref[ZERO_ROW * PARTS :] = jnp.zeros((PARTS, 8, WIDE), BF16)
    smalls[7].wait()
    for copy in copies[:4]:
        copy.wait_recv()
    scalars_ref[:NODES, :] = nodes_ref[:, :C]
    scalars_ref[NODES:, :] = arrived_ref[:, :C]
    harmonic_sums(
        across_refs,
        harm_ref,
        scalars_ref,
        gate0_ref,
        rows_ref,
        turned_ref,
        harm_rows_ref,
        harm_sums_ref,
        first_ref,
    )
    for copy in copies[4:]:
        copy.wait_recv()
    spread_rows(arrived_ref, 4 * HALO, NODES, wide_ref, table_ref)
    for copy in copies:
        copy.wait_send()


def sum_edges(slots, table_ref, gates_ref, sums_ref):
    @pl.loop(0, BLOCKS)
    def _(b):
        first = slots[b, SLOTS]
        total0 = jnp.zeros((PARTS, 8, WIDE), F32)
        total1 = jnp.zeros((PARTS, 8, WIDE), F32)
        for j in range(CHUNKS):
            parts = []
            for k in range(CHUNK):
                at = j * CHUNK + k
                parts.append(
                    table_ref[pl.ds(slots[b, at], PARTS)] * gates_ref[pl.ds(slots[b, HALF + at], PARTS)]
                )
            part = ((parts[0] + parts[1]) + (parts[2] + parts[3])).astype(F32)
            mine = j < first
            total0 = total0 + jnp.where(mine, part, 0.0)
            total1 = total1 + jnp.where(mine, 0.0, part)
        at = pl.multiple_of(b * (2 * ROWS), 8)
        for t, total in enumerate((total0, total1)):
            for tile in range(6):
                i, h = divmod(tile, 2)
                sums_ref[pl.ds(at + t * ROWS + 8 * tile, 8), :] = total[i, :, h * C : (h + 1) * C]


def update_nodes(nodes_ref, sums_ref, first_ref, harm_sums_ref, weight_ref, squares_ref, combined_ref):
    squares_ref[...] = jnp.zeros((NODES, C), F32)

    def one(lm, degree, left):
        left = jnp.concatenate([left, harm_sums_ref[lm]], axis=1).astype(BF16)
        mixed = jnp.dot(left, weight_ref[degree], preferred_element_type=F32)
        cut = pl.ds(pl.multiple_of(lm * C, C), C)
        value = nodes_ref[:, cut].astype(F32) + mixed
        combined_ref[:, cut] = value
        squares_ref[...] += value * value

    one(0, 0, first_ref[...])

    @pl.loop(0, 12)
    def _(step):
        for n in range(4):
            lm = step * 4 + n + 1
            degree = 1
            for d in range(2, DEG):
                degree = degree + (lm >= d * d).astype(I32)
            one(lm, degree, sums_ref[pl.ds(lm - 1, NODES, stride=ROWS), :])


def layer_kernel(
    table_ref,
    gates_ref,
    harm_sums_ref,
    first_ref,
    slot_ref,
    mix_ref,
    harmonic_ref,
    update_ref,
    gain_ref,
    nodes_ref,
    out_hbm,
    slots,
    weight_ref,
    sums_ref,
    squares_ref,
    combined_ref,
    out_ref,
    slot_sem,
    out_sem,
):
    slot_copy = pltpu.make_async_copy(slot_ref, slots, slot_sem)
    slot_copy.start()
    for degree in range(DEG):
        both = jnp.concatenate([mix_ref[degree], harmonic_ref[...]], axis=0)
        weight_ref[degree] = jnp.dot(both, update_ref[degree], preferred_element_type=F32).astype(BF16)
    slot_copy.wait()
    sum_edges(slots, table_ref, gates_ref, sums_ref)
    update_nodes(nodes_ref, sums_ref, first_ref, harm_sums_ref, weight_ref, squares_ref, combined_ref)
    mean = jnp.sum(squares_ref[...], axis=1, keepdims=True) / FEAT
    squares_ref[...] = jnp.broadcast_to(lax.rsqrt(mean + norm_eps), (NODES, C))
    copies = []
    for c in range(PIECES):
        for lm in range(7 * c, 7 * c + 7, 2):
            pair = []
            for at in range(lm, min(lm + 2, 7 * c + 7)):
                degree = int(DEGREE_OF[at])
                pair.append(
                    combined_ref[:, at * C : (at + 1) * C]
                    * squares_ref[...]
                    * gain_ref[degree : degree + 1, :]
                )
            value = jnp.concatenate(pair, axis=1) if len(pair) == 2 else pair[0]
            out_ref[:, lm * C : (lm + len(pair)) * C] = value.astype(BF16)
        cut = pl.ds(c * PIECE, PIECE)
        copy = pltpu.make_async_copy(out_ref.at[:, cut], out_hbm.at[:, cut], out_sem.at[c])
        copy.start()
        copies.append(copy)
    for copy in copies:
        copy.wait()


VMEM = pl.BlockSpec(memory_space=pltpu.VMEM)
ANY = pl.BlockSpec(memory_space=pl.ANY)
HBM = pl.BlockSpec(memory_space=pltpu.HBM)


def gather(*arrays, peers, columns):
    return pl.pallas_call(
        functools.partial(gather_kernel, peers=peers, columns=columns),
        out_shape=(
            pltpu.VMEM(((TABLE + 1) * PARTS, 8, WIDE), BF16),
            pltpu.VMEM((LENGTHS * PARTS, 8, WIDE), BF16),
            pltpu.VMEM((COEF, NODES, C), F32),
            pltpu.VMEM((NODES, C), F32),
            pltpu.VMEM((BLOCKS, 2 * HALF), I32),
        ),
        in_specs=[HBM] * 9,
        out_specs=(VMEM,) * 5,
        scratch_shapes=[
            pltpu.VMEM((4, HALO), I32),
            pltpu.VMEM((1, BLOCKS - KEEP), I32),
            pltpu.VMEM((EB, BLOCKS), I32),
            pltpu.VMEM((EB, BLOCKS), I32),
            pltpu.VMEM((EB, BLOCKS), BF16),
            pltpu.VMEM((HID, RB), BF16),
            pltpu.VMEM((COEF, EB, BLOCKS), BF16),
            pltpu.VMEM((NODES, FEAT), BF16),
            pltpu.VMEM((HID, DEG * C), BF16),
            pltpu.VMEM((4 * HALO, FEAT), BF16),
            pltpu.VMEM((4 * HALO, FEAT), BF16),
            pltpu.VMEM((LENGTHS, DEG * C), F32),
            pltpu.VMEM((LENGTHS, C), BF16),
            pltpu.VMEM((16 * ROWS, C), F32),
            pltpu.VMEM((TABLE, C), BF16),
            pltpu.VMEM((BLOCKS, EB), I32),
            pltpu.VMEM((BLOCKS, EB), I32),
            pltpu.VMEM((BLOCKS, EB), I32),
            pltpu.VMEM((3, GROUPS, GE), I32),
            pltpu.VMEM((7, BLOCKS, EB), F32),
            pltpu.VMEM((COEF * GROUPS, GE), F32),
            pltpu.SemaphoreType.DMA((PIECES,)),
            pltpu.SemaphoreType.DMA((8,)),
            pltpu.SemaphoreType.DMA((4, PIECES)),
            pltpu.SemaphoreType.DMA((4, PIECES)),
        ],
        compiler_params=pltpu.CompilerParams(
            collective_id=0, has_side_effects=True, vmem_limit_bytes=GATHER_VMEM
        ),
        name="gather",
    )(*[pltpu.with_memory_space_constraint(a, pltpu.HBM) for a in arrays])


def layer(table, gates, harm_sums, first, slot, mix, harmonic, update, gain, nodes):
    return pl.pallas_call(
        layer_kernel,
        out_shape=jax.ShapeDtypeStruct((NODES, FEAT), BF16),
        in_specs=[VMEM] * 10,
        out_specs=ANY,
        scratch_shapes=[
            pltpu.SMEM((BLOCKS, 2 * HALF), I32),
            pltpu.VMEM((DEG, 2 * C, C), BF16),
            pltpu.VMEM((NODES * ROWS, C), F32),
            pltpu.VMEM((NODES, C), F32),
            pltpu.VMEM((NODES, FEAT), F32),
            pltpu.VMEM((NODES, FEAT), BF16),
            pltpu.SemaphoreType.DMA,
            pltpu.SemaphoreType.DMA((PIECES,)),
        ],
        compiler_params=pltpu.CompilerParams(vmem_limit_bytes=LAYER_VMEM),
        name="layer",
    )(table, gates, harm_sums, first, slot, mix, harmonic, update, gain, nodes)


GATHER_VMEM = 22 * 1024 * 1024
LAYER_VMEM = 26 * 1024 * 1024


def per_device(
    node_feats,
    halo_index,
    edge_source,
    edge_target,
    edge_length,
    edge_harmonics,
    block_peer,
    radial_in,
    radial_out,
    mix_weight,
    harmonic_weight,
    update_weight,
    norm_gain,
):
    gathered = gather(
        node_feats,
        halo_index[0],
        block_peer,
        edge_source.T,
        edge_target.T,
        edge_length.T,
        radial_in.T,
        radial_out,
        edge_harmonics.transpose(2, 1, 0),
        peers=lax.axis_size("gx"),
        columns=lax.axis_size("gy"),
    )
    return layer(*gathered, mix_weight, harmonic_weight, update_weight, norm_gain, node_feats)


def solution(mesh):
    split = ("gx", "gy")
    in_specs = (
        P(split, None),
        P(split, None, None),
        P(split, None),
        P(split, None),
        P(split, None),
        P(split, None, None),
        P(split, None),
        P(),
        P(),
        P(),
        P(),
        P(),
        P(),
    )
    return jax.shard_map(
        per_device, mesh=mesh, in_specs=in_specs, out_specs=P(split, None), check_vma=False
    )
```

time: 78.5 us -> 45.8 us (0.58)
  local copies, waits for them, and re-layouts: 10.6 us -> 0.02 us
  Pallas kernels: 55.4 us -> 45.6 us
  starting transfers between devices: 8.49 us -> 0 us
  waiting for transfers between devices: 2.38 us -> 0 us
  other arithmetic: 1.25 us -> 0 us
    pallas_call x1, Pallas kernels: 54.7 us -> 20.8 us  [layer(): pl.pallas_call(layer_kernel, out_shape=jax.ShapeDtypeStruct((NODES, FEAT)...]
    pallas_call x1, Pallas kernels: 0.69 us -> 24.9 us  [gather(): pl.pallas_call(functools.partial(gather_kernel, peers=peers, columns=colu...]
    ppermute x4 -> x0, starting transfers between devices: 8.49 us -> none  [shifted(): lax.ppermute(rows, axis, [((i - step) % size, i) for i in range(size)])]
    reshape x8 -> x0, local copies, waits for them, and re-layouts: 5.12 us -> none  [the longest x2 1.99 us: edge_lists(): harm = edge_harmonics.reshape(GROUPS, GE, COEF).transpose(0, 2, 1)]
    unnamed x17 -> x10, local copies, waits for them, and re-layouts: 4.34 us -> 0.02 us
    ppermute x4 -> x0, waiting for transfers between devices: 2.38 us -> none  [shifted(): lax.ppermute(rows, axis, [((i - step) % size, i) for i in range(size)])]
    transpose x2 -> x0, other arithmetic: 1.22 us -> none  [edge_lists(): return (payload.T, target.T, edge_source.reshape(GROUPS, GE).T, length.re...]
    slice x1 -> x0, local copies, waits for them, and re-layouts: 0.86 us -> none  [per_device(): outgoing[HALO * k:HALO * (k + 1)]]
  transfers between devices with their start and end apart: 4 -> 0, of which waited for: 1 -> 0; matrix products, arithmetic and copies ran while one was open for 11% -> 0% of each run, Pallas kernels for 0% -> 0%
where the time goes in v2:
time: 45.8 us; the launch traced here: 45.7 us
  Pallas kernels  45.6 us (100%)
    pallas_call x1, Pallas kernels, gather(): pl.pallas_call(functools.partial(gather_kernel, peers=peers, columns=colu...  24.9 us
    pallas_call x1, Pallas kernels, layer(): pl.pallas_call(layer_kernel, out_shape=jax.ShapeDtypeStruct((NODES, FEAT)...  20.8 us

profile of v2, /device:TPU:0, one launch (start us, length us, event | category | flops | bytes accessed | tf_op | source)
XLA Modules:
  0.0 45.7 jit_solution(3605930049000809830)
XLA Ops:
  0.0 0.0 copy-start
  0.0 0.0 copy-start.4
  0.0 0.0 copy-start.2
  0.0 0.0 copy-start.3
  0.0 0.0 copy-start.1
  0.0 24.9 %gather.1 = (bf16[1155,8,256]{2,1,0:T(8,128)(2,1)S(1)}, bf16[1152,8,256]{2,1,0:T(8,128)(2,1)S(1)}, f32[49,256,128]{2,1,0:T(8,128)S(1)}, f32[256,128]{1,0:T(8,128)S(1)}, s32[128,128]{1,0:T(8,128)S(1)}) custom-call(bf16[256,6272]{1,0:T(8,128)(2,1)} %nodes_ref.1, s32[4,32]{1,0:T(4,128)} %bitcast.11, s32[1,32]{1,0:T(1,128)} %peer_hbm.1, s32[32,128]{1,0:T(8,128)} %bitcast.8, ...), custom_call_target="tpu_custom_call" | custom-call | tf_op jit(solution)/shard_map/gather/pallas_call | solution.py:461
  24.9 0.0 copy-done
  24.9 0.0 copy-done.4
  24.9 0.0 copy-done.2
  24.9 0.0 copy-done.3
  24.9 0.0 copy-done.1
  24.9 20.8 %layer.1 = bf16[256,6272]{1,0:T(8,128)(2,1)} custom-call(bf16[1155,8,256]{2,1,0:T(8,128)(2,1)S(1)} %get-tuple-element.10.table_ref, bf16[1152,8,256]{2,1,0:T(8,128)(2,1)S(1)} %get-tuple-element.11.gates_ref, f32[49,256,128]{2,1,0:T(8,128)S(1)} %get-tuple-element.12.harm_sums_ref, f32[256,128]{1,0:T(8,128)S(1)} %get-tuple-element.13.first_ref, ...), custom_call_target="tpu_custom_call" | custom-call | tf_op jit(solution)/shard_map/layer/pallas_call | solution.py:507
Async XLA Ops:
  0.0 24.9 %copy-start = (bf16[256,6272]{1,0:T(8,128)(2,1)S(1)}, bf16[256,6272]{1,0:T(8,128)(2,1)}, u32[]{:S(2)}) copy-start(bf16[256,6272]{1,0:T(8,128)(2,1)} %nodes_ref.1) | copy-start | bytes 9633796
  0.0 24.9 %copy-start.4 = (f32[7,128]{1,0:T(8,128)S(1)}, f32[7,128]{1,0:T(8,128)}, u32[]{:S(2)}) copy-start(f32[7,128]{1,0:T(8,128)} %gain_ref.1) | copy-start | bytes 10756
  0.0 24.9 %copy-start.2 = (bf16[7,128,128]{2,1,0:T(8,128)(2,1)S(1)}, bf16[7,128,128]{2,1,0:T(8,128)(2,1)}, u32[]{:S(2)}) copy-start(bf16[7,128,128]{2,1,0:T(8,128)(2,1)} %update_ref.1) | copy-start | bytes 688132
  0.0 24.9 %copy-start.3 = (bf16[128,128]{1,0:T(8,128)(2,1)S(1)}, bf16[128,128]{1,0:T(8,128)(2,1)}, u32[]{:S(2)}) copy-start(bf16[128,128]{1,0:T(8,128)(2,1)} %harmonic_ref.1) | copy-start | bytes 98308
  0.0 24.9 %copy-start.1 = (bf16[7,128,128]{2,1,0:T(8,128)(2,1)S(1)}, bf16[7,128,128]{2,1,0:T(8,128)(2,1)}, u32[]{:S(2)}) copy-start(bf16[7,128,128]{2,1,0:T(8,128)(2,1)} %mix_ref.1) | copy-start | bytes 688132

commit v3 on v2

--- a/solution.py
+++ b/solution.py
@@ -43,7 +43,9 @@
 DEGREE_OF = np.repeat(np.arange(LMAX + 1), 2 * np.arange(LMAX + 1) + 1)
 PARTS = 3
 WIDE = 2 * C
-HALF = 64
+LISTS = 80
+STEP = 8
+BAND = 32
 PIECE = 7 * C
 PIECES = FEAT // PIECE
 MESH = pl.DeviceIdType.MESH
@@ -81,7 +83,8 @@
     k = lax.broadcasted_iota(I32, (LENGTHS, RB), 1).astype(F32)
     centers = cutoff_radius * (k + 0.5) / RB
     spread = 2.0 * cutoff_radius / RB
-    envelope = 0.5 * (jnp.cos(jnp.pi * r / cutoff_radius) + 1.0)
+    along = length_of(lax.broadcasted_iota(I32, (8, LENGTHS), 1).astype(F32))
+    envelope = (0.5 * (jnp.cos(jnp.pi * along / cutoff_radius) + 1.0)).T[:, :1]
     offsets = (r - centers) / spread
     basis = (jnp.exp(-0.5 * offsets * offsets) * envelope).astype(BF16)
     hidden = lax.dot_general(
@@ -159,11 +162,10 @@
     for s in range(SLOTS):
         rows.append(jnp.sum(jnp.where(slot == s, relative, 0), axis=0, keepdims=True) + ZERO_ROW * PARTS)
     rows.append(lax.shift_right_logical(count0 + (CHUNK - 1), 2))
-    rows.append(jnp.zeros((HALF - SLOTS - 1, BLOCKS), I32))
     for s in range(SLOTS):
         rows.append(jnp.sum(jnp.where(slot == s, length, 0), axis=0, keepdims=True))
-    rows.append(jnp.zeros((HALF - SLOTS, BLOCKS), I32))
-    slot_ref[...] = jnp.concatenate(rows, axis=0).T
+    rows.append(jnp.zeros((LISTS - 2 * SLOTS - 1, BLOCKS), I32))
+    slot_ref[...] = jnp.concatenate(rows, axis=0)
 
 
 def by_group(ref):
@@ -178,8 +180,8 @@
     return lax.dot_general(identity, x, (((1,), (1,)), ((), ())), preferred_element_type=F32)
 
 
-def harmonic_sums(
-    across_refs, harm_ref, scalars_ref, gate0_ref, rows_ref, turned_ref, harm_rows_ref, harm_sums_ref, first_ref
+def turn_harmonics(
+    across_refs, harm_ref, scalars_ref, gate0_ref, turned_ref, rows_ref, harm_rows_ref, zeroth_ref
 ):
     for n, ref in enumerate(across_refs):
         rows_ref[n] = by_group(ref)
@@ -191,36 +193,28 @@
             at = pl.multiple_of((step * 7 + n) * GROUPS, GROUPS)
             harm_rows_ref[pl.ds(at, GROUPS), :] = by_group(turned_ref.at[n])
 
-    node = lax.broadcasted_iota(I32, (GN, GE), 0)
-    edge = lax.broadcasted_iota(I32, (GN, GE), 1)
-    same_block = lax.shift_right_logical(node, 1) == lax.shift_right_logical(edge, 5)
-    wanted = jnp.where(same_block, lax.bitwise_and(node, 1), -1)
+    zeroth_ref[1] = transposed(gate0_ref[...]).astype(BF16)
+
+
+def harmonic_sums(g, wanted, rows_ref, harm_rows_ref, zeroth_ref, harm_sums_ref, first_ref):
     across = (((1,), (1,)), ((), ()))
-    scalars = transposed(scalars_ref[...]).astype(BF16)
-    gate0 = transposed(gate0_ref[...]).astype(BF16)
-
-    @pl.loop(0, GROUPS)
-    def _(g):
-        row = lax.broadcasted_iota(I32, (TABLE, GE), 0)
-        pick = (rows_ref[0, pl.ds(g, 1), :] == row).astype(F32).astype(BF16)
-        scalar = jnp.dot(scalars, pick, preferred_element_type=F32).astype(BF16)
-        pick = (rows_ref[1, pl.ds(g, 1), :] == row).astype(F32).astype(BF16)
-        gate = jnp.dot(gate0, pick, preferred_element_type=F32).astype(BF16)
-        mask = (rows_ref[2, pl.ds(g, 1), :] == wanted).astype(F32)
-        at = pl.multiple_of(g * GN, GN)
-        first_ref[pl.ds(at, GN), :] = lax.dot_general(
-            mask.astype(BF16), scalar * gate, across, preferred_element_type=F32
-        )
-        left = jnp.concatenate(
-            [
-                (harm_rows_ref[pl.ds(lm * GROUPS + g, 1), :] * mask).astype(BF16)
-                for lm in range(COEF)
-            ],
-            axis=0,
-        )
-        right = lax.dot_general(left, scalar, across, preferred_element_type=F32)
-        for lm in range(COEF):
-            harm_sums_ref[lm, pl.ds(at, GN), :] = right[lm * GN : (lm + 1) * GN]
+    row = lax.broadcasted_iota(I32, (TABLE, GE), 0)
+    pick = (rows_ref[0, pl.ds(g, 1), :] == row).astype(F32).astype(BF16)
+    scalar = jnp.dot(zeroth_ref[0], pick, preferred_element_type=F32).astype(BF16)
+    pick = (rows_ref[1, pl.ds(g, 1), :] == row).astype(F32).astype(BF16)
+    gate = jnp.dot(zeroth_ref[1], pick, preferred_element_type=F32).astype(BF16)
+    mask = (rows_ref[2, pl.ds(g, 1), :] == wanted).astype(F32)
+    at = pl.multiple_of(g * GN, GN)
+    first_ref[pl.ds(at, GN), :] = lax.dot_general(
+        mask.astype(BF16), scalar * gate, across, preferred_element_type=F32
+    )
+    left = jnp.concatenate(
+        [(harm_rows_ref[pl.ds(lm * GROUPS + g, 1), :] * mask).astype(BF16) for lm in range(COEF)],
+        axis=0,
+    )
+    right = lax.dot_general(left, scalar, across, preferred_element_type=F32)
+    for lm in range(COEF):
+        harm_sums_ref[lm, pl.ds(at, GN), :] = right[lm * GN : (lm + 1) * GN]
 
 
 def gather_kernel(
@@ -233,11 +227,16 @@
     radial_in_hbm,
     radial_out_hbm,
     harm_hbm,
+    mix_hbm,
+    harmonic_hbm,
+    update_hbm,
     table_ref,
     gates_ref,
-    harm_sums_ref,
-    first_ref,
+    rows_ref,
+    harm_rows_ref,
+    zeroth_ref,
     slot_ref,
+    weight_ref,
     halo_ref,
     peer_ref,
     source_ref,
@@ -245,6 +244,9 @@
     length_ref,
     radial_in_ref,
     harm_ref,
+    mix_ref,
+    harmonic_ref,
+    update_ref,
     nodes_ref,
     radial_out_ref,
     send_ref,
@@ -256,9 +258,7 @@
     source_across_ref,
     length_across_ref,
     target_across_ref,
-    rows_ref,
     turned_ref,
-    harm_rows_ref,
     load_sem,
     other_sem,
     send_sem,
@@ -282,6 +282,9 @@
             (radial_in_hbm, radial_in_ref),
             (radial_out_hbm, radial_out_ref),
             (harm_hbm, harm_ref),
+            (mix_hbm, mix_ref),
+            (harmonic_hbm, harmonic_ref),
+            (update_hbm, update_ref),
         )
     ):
         smalls.append(pltpu.make_async_copy(source, target, other_sem.at[n]))
@@ -331,125 +334,142 @@
     spread_rows(nodes_ref, NODES, 0, wide_ref, table_ref)
     table_ref[ZERO_ROW * PARTS :] = jnp.zeros((PARTS, 8, WIDE), BF16)
     smalls[7].wait()
-    for copy in copies[:4]:
+    turn_harmonics(
+        across_refs, harm_ref, scalars_ref, gate0_ref, turned_ref, rows_ref, harm_rows_ref, zeroth_ref
+    )
+    for load in smalls[8:]:
+        load.wait()
+    for degree in range(DEG):
+        both = jnp.concatenate([mix_ref[degree], harmonic_ref[...]], axis=0)
+        weight_ref[degree] = jnp.dot(both, update_ref[degree], preferred_element_type=F32).astype(BF16)
+    for copy in copies:
         copy.wait_recv()
+    spread_rows(arrived_ref, 4 * HALO, NODES, wide_ref, table_ref)
     scalars_ref[:NODES, :] = nodes_ref[:, :C]
     scalars_ref[NODES:, :] = arrived_ref[:, :C]
-    harmonic_sums(
-        across_refs,
-        harm_ref,
-        scalars_ref,
-        gate0_ref,
-        rows_ref,
-        turned_ref,
-        harm_rows_ref,
-        harm_sums_ref,
-        first_ref,
-    )
-    for copy in copies[4:]:
-        copy.wait_recv()
-    spread_rows(arrived_ref, 4 * HALO, NODES, wide_ref, table_ref)
+    zeroth_ref[0] = transposed(scalars_ref[...]).astype(BF16)
     for copy in copies:
         copy.wait_send()
 
 
-def sum_edges(slots, table_ref, gates_ref, sums_ref):
-    @pl.loop(0, BLOCKS)
-    def _(b):
-        first = slots[b, SLOTS]
-        total0 = jnp.zeros((PARTS, 8, WIDE), F32)
-        total1 = jnp.zeros((PARTS, 8, WIDE), F32)
-        for j in range(CHUNKS):
-            parts = []
-            for k in range(CHUNK):
-                at = j * CHUNK + k
-                parts.append(
-                    table_ref[pl.ds(slots[b, at], PARTS)] * gates_ref[pl.ds(slots[b, HALF + at], PARTS)]
-                )
-            part = ((parts[0] + parts[1]) + (parts[2] + parts[3])).astype(F32)
-            mine = j < first
-            total0 = total0 + jnp.where(mine, part, 0.0)
-            total1 = total1 + jnp.where(mine, 0.0, part)
-        at = pl.multiple_of(b * (2 * ROWS), 8)
-        for t, total in enumerate((total0, total1)):
-            for tile in range(6):
-                i, h = divmod(tile, 2)
-                sums_ref[pl.ds(at + t * ROWS + 8 * tile, 8), :] = total[i, :, h * C : (h + 1) * C]
+def sum_edges(b, slots, table_ref, gates_ref, sums_ref):
+    first = slots[SLOTS][b]
+    total0 = jnp.zeros((PARTS, 8, WIDE), F32)
+    running = jnp.zeros((PARTS, 8, WIDE), F32)
+    for j in range(CHUNKS):
+        parts = []
+        for k in range(CHUNK):
+            at = j * CHUNK + k
+            parts.append(
+                table_ref[pl.ds(slots[at][b], PARTS)] * gates_ref[pl.ds(slots[SLOTS + 1 + at][b], PARTS)]
+            )
+        part = ((parts[0] + parts[1]) + (parts[2] + parts[3])).astype(F32)
+        running = running + part
+        total0 = jnp.where(j < first, running, total0)
+    at = pl.multiple_of(b * (2 * ROWS), 8)
+    for t, total in enumerate((total0, running - total0)):
+        for tile in range(6):
+            i, h = divmod(tile, 2)
+            sums_ref[pl.ds(at + t * ROWS + 8 * tile, 8), :] = total[i, :, h * C : (h + 1) * C]
+
+
+def sum_blocks(slots, rows_ref, harm_rows_ref, zeroth_ref, table_ref, gates_ref, sums_ref, harm_sums_ref, first_ref):
+    node = lax.broadcasted_iota(I32, (GN, GE), 0)
+    edge = lax.broadcasted_iota(I32, (GN, GE), 1)
+    same_block = lax.shift_right_logical(node, 1) == lax.shift_right_logical(edge, 5)
+    wanted = jnp.where(same_block, lax.bitwise_and(node, 1), -1)
+
+    @pl.loop(0, GROUPS)
+    def _(g):
+        harmonic_sums(g, wanted, rows_ref, harm_rows_ref, zeroth_ref, harm_sums_ref, first_ref)
+        for n in range(GROUP):
+            sum_edges(g * GROUP + n, slots, table_ref, gates_ref, sums_ref)
 
 
 def update_nodes(nodes_ref, sums_ref, first_ref, harm_sums_ref, weight_ref, squares_ref, combined_ref):
-    squares_ref[...] = jnp.zeros((NODES, C), F32)
-
     def one(lm, degree, left):
         left = jnp.concatenate([left, harm_sums_ref[lm]], axis=1).astype(BF16)
         mixed = jnp.dot(left, weight_ref[degree], preferred_element_type=F32)
         cut = pl.ds(pl.multiple_of(lm * C, C), C)
         value = nodes_ref[:, cut].astype(F32) + mixed
         combined_ref[:, cut] = value
-        squares_ref[...] += value * value
-
-    one(0, 0, first_ref[...])
-
-    @pl.loop(0, 12)
+        return value * value
+
+    squares_ref[...] = one(0, 0, first_ref[...])
+
+    @pl.loop(0, 48 // STEP)
     def _(step):
-        for n in range(4):
-            lm = step * 4 + n + 1
+        squares = None
+        for n in range(STEP):
+            lm = step * STEP + n + 1
             degree = 1
             for d in range(2, DEG):
                 degree = degree + (lm >= d * d).astype(I32)
-            one(lm, degree, sums_ref[pl.ds(lm - 1, NODES, stride=ROWS), :])
+            square = one(lm, degree, sums_ref[pl.ds(lm - 1, NODES, stride=ROWS), :])
+            squares = square if squares is None else squares + square
+        squares_ref[...] += squares
+
+
+def store_nodes(squares_ref, gain_ref, combined_ref, out_ref, out_hbm, out_sem):
+    mean = jnp.sum(squares_ref[...], axis=1, keepdims=True) / FEAT
+    squares_ref[...] = jnp.broadcast_to(lax.rsqrt(mean + norm_eps), (NODES, C))
+
+    def copy(n):
+        cut = pl.ds(pl.multiple_of(n * BAND, BAND), BAND)
+        return pltpu.make_async_copy(out_ref.at[cut], out_hbm.at[cut], out_sem.at[n])
+
+    @pl.loop(0, NODES // BAND)
+    def _(n):
+        cut = pl.ds(pl.multiple_of(n * BAND, BAND), BAND)
+        inverse = squares_ref[cut, :]
+        for lm in range(0, COEF, 2):
+            pair = []
+            for at in range(lm, min(lm + 2, COEF)):
+                degree = int(DEGREE_OF[at])
+                pair.append(
+                    combined_ref[cut, at * C : (at + 1) * C] * inverse * gain_ref[degree : degree + 1, :]
+                )
+            value = jnp.concatenate(pair, axis=1) if len(pair) == 2 else pair[0]
+            out_ref[cut, lm * C : (lm + len(pair)) * C] = value.astype(BF16)
+        copy(n).start()
+
+    for n in range(NODES // BAND):
+        copy(n).wait()
 
 
 def layer_kernel(
     table_ref,
     gates_ref,
-    harm_sums_ref,
-    first_ref,
+    rows_ref,
+    harm_rows_ref,
+    zeroth_ref,
     slot_ref,
-    mix_ref,
-    harmonic_ref,
-    update_ref,
+    weight_ref,
     gain_ref,
     nodes_ref,
     out_hbm,
-    slots,
-    weight_ref,
     sums_ref,
+    harm_sums_ref,
+    first_ref,
     squares_ref,
     combined_ref,
     out_ref,
     slot_sem,
     out_sem,
+    *slots,
 ):
-    slot_copy = pltpu.make_async_copy(slot_ref, slots, slot_sem)
-    slot_copy.start()
-    for degree in range(DEG):
-        both = jnp.concatenate([mix_ref[degree], harmonic_ref[...]], axis=0)
-        weight_ref[degree] = jnp.dot(both, update_ref[degree], preferred_element_type=F32).astype(BF16)
-    slot_copy.wait()
-    sum_edges(slots, table_ref, gates_ref, sums_ref)
+    slot_copies = []
+    for n, slot in enumerate(slots):
+        copy = pltpu.make_async_copy(slot_ref.at[n], slot, slot_sem.at[n])
+        copy.start()
+        slot_copies.append(copy)
+    for copy in slot_copies:
+        copy.wait()
+    sum_blocks(
+        slots, rows_ref, harm_rows_ref, zeroth_ref, table_ref, gates_ref, sums_ref, harm_sums_ref, first_ref
+    )
     update_nodes(nodes_ref, sums_ref, first_ref, harm_sums_ref, weight_ref, squares_ref, combined_ref)
-    mean = jnp.sum(squares_ref[...], axis=1, keepdims=True) / FEAT
-    squares_ref[...] = jnp.broadcast_to(lax.rsqrt(mean + norm_eps), (NODES, C))
-    copies = []
-    for c in range(PIECES):
-        for lm in range(7 * c, 7 * c + 7, 2):
-            pair = []
-            for at in range(lm, min(lm + 2, 7 * c + 7)):
-                degree = int(DEGREE_OF[at])
-                pair.append(
-                    combined_ref[:, at * C : (at + 1) * C]
-                    * squares_ref[...]
-                    * gain_ref[degree : degree + 1, :]
-                )
-            value = jnp.concatenate(pair, axis=1) if len(pair) == 2 else pair[0]
-            out_ref[:, lm * C : (lm + len(pair)) * C] = value.astype(BF16)
-        cut = pl.ds(c * PIECE, PIECE)
-        copy = pltpu.make_async_copy(out_ref.at[:, cut], out_hbm.at[:, cut], out_sem.at[c])
-        copy.start()
-        copies.append(copy)
-    for copy in copies:
-        copy.wait()
+    store_nodes(squares_ref, gain_ref, combined_ref, out_ref, out_hbm, out_sem)
 
 
 VMEM = pl.BlockSpec(memory_space=pltpu.VMEM)
@@ -463,12 +483,14 @@
         out_shape=(
             pltpu.VMEM(((TABLE + 1) * PARTS, 8, WIDE), BF16),
             pltpu.VMEM((LENGTHS * PARTS, 8, WIDE), BF16),
-            pltpu.VMEM((COEF, NODES, C), F32),
-            pltpu.VMEM((NODES, C), F32),
-            pltpu.VMEM((BLOCKS, 2 * HALF), I32),
+            pltpu.VMEM((3, GROUPS, GE), I32),
+            pltpu.VMEM((COEF * GROUPS, GE), F32),
+            pltpu.VMEM((2, C, TABLE), BF16),
+            pltpu.VMEM((LISTS, BLOCKS), I32),
+            pltpu.VMEM((DEG, 2 * C, C), BF16),
         ),
-        in_specs=[HBM] * 9,
-        out_specs=(VMEM,) * 5,
+        in_specs=[HBM] * 12,
+        out_specs=(VMEM,) * 7,
         scratch_shapes=[
             pltpu.VMEM((4, HALO), I32),
             pltpu.VMEM((1, BLOCKS - KEEP), I32),
@@ -477,6 +499,9 @@
             pltpu.VMEM((EB, BLOCKS), BF16),
             pltpu.VMEM((HID, RB), BF16),
             pltpu.VMEM((COEF, EB, BLOCKS), BF16),
+            pltpu.VMEM((DEG, C, C), BF16),
+            pltpu.VMEM((C, C), BF16),
+            pltpu.VMEM((DEG, C, C), BF16),
             pltpu.VMEM((NODES, FEAT), BF16),
             pltpu.VMEM((HID, DEG * C), BF16),
             pltpu.VMEM((4 * HALO, FEAT), BF16),
@@ -488,11 +513,9 @@
             pltpu.VMEM((BLOCKS, EB), I32),
             pltpu.VMEM((BLOCKS, EB), I32),
             pltpu.VMEM((BLOCKS, EB), I32),
-            pltpu.VMEM((3, GROUPS, GE), I32),
             pltpu.VMEM((7, BLOCKS, EB), F32),
-            pltpu.VMEM((COEF * GROUPS, GE), F32),
             pltpu.SemaphoreType.DMA((PIECES,)),
-            pltpu.SemaphoreType.DMA((8,)),
+            pltpu.SemaphoreType.DMA((11,)),
             pltpu.SemaphoreType.DMA((4, PIECES)),
             pltpu.SemaphoreType.DMA((4, PIECES)),
         ],
@@ -503,29 +526,30 @@
     )(*[pltpu.with_memory_space_constraint(a, pltpu.HBM) for a in arrays])
 
 
-def layer(table, gates, harm_sums, first, slot, mix, harmonic, update, gain, nodes):
+def layer(*arrays):
     return pl.pallas_call(
         layer_kernel,
         out_shape=jax.ShapeDtypeStruct((NODES, FEAT), BF16),
-        in_specs=[VMEM] * 10,
+        in_specs=[VMEM] * len(arrays),
         out_specs=ANY,
         scratch_shapes=[
-            pltpu.SMEM((BLOCKS, 2 * HALF), I32),
-            pltpu.VMEM((DEG, 2 * C, C), BF16),
             pltpu.VMEM((NODES * ROWS, C), F32),
+            pltpu.VMEM((COEF, NODES, C), F32),
+            pltpu.VMEM((NODES, C), F32),
             pltpu.VMEM((NODES, C), F32),
             pltpu.VMEM((NODES, FEAT), F32),
             pltpu.VMEM((NODES, FEAT), BF16),
-            pltpu.SemaphoreType.DMA,
-            pltpu.SemaphoreType.DMA((PIECES,)),
-        ],
+            pltpu.SemaphoreType.DMA((2 * SLOTS + 1,)),
+            pltpu.SemaphoreType.DMA((NODES // BAND,)),
+        ]
+        + [pltpu.SMEM((BLOCKS,), I32)] * (2 * SLOTS + 1),
         compiler_params=pltpu.CompilerParams(vmem_limit_bytes=LAYER_VMEM),
         name="layer",
-    )(table, gates, harm_sums, first, slot, mix, harmonic, update, gain, nodes)
+    )(*arrays)
 
 
 GATHER_VMEM = 22 * 1024 * 1024
-LAYER_VMEM = 26 * 1024 * 1024
+LAYER_VMEM = 30 * 1024 * 1024
 
 
 def per_device(
@@ -553,10 +577,13 @@
         radial_in.T,
         radial_out,
         edge_harmonics.transpose(2, 1, 0),
+        mix_weight,
+        harmonic_weight,
+        update_weight,
         peers=lax.axis_size("gx"),
         columns=lax.axis_size("gy"),
     )
-    return layer(*gathered, mix_weight, harmonic_weight, update_weight, norm_gain, node_feats)
+    return layer(*gathered, norm_gain, node_feats)
 
 
 def solution(mesh):

time: 45.8 us -> 40.8 us (0.89)
  Pallas kernels: 45.6 us -> 40.7 us
    pallas_call x1, Pallas kernels: 24.9 us -> 17 us  [gather(): pl.pallas_call(functools.partial(gather_kernel, peers=peers, columns=colu...]
    pallas_call x1, Pallas kernels: 20.8 us -> 23.7 us  [layer(): pl.pallas_call(layer_kernel, out_shape=jax.ShapeDtypeStruct((NODES, FEAT)...]
where the time goes in v3:
time: 40.8 us; the launch traced here: 40.7 us
  Pallas kernels  40.7 us (100%)
    pallas_call x1, Pallas kernels, layer(): pl.pallas_call(layer_kernel, out_shape=jax.ShapeDtypeStruct((NODES, FEAT)...  23.7 us
    pallas_call x1, Pallas kernels, gather(): pl.pallas_call(functools.partial(gather_kernel, peers=peers, columns=colu...  17 us

profile of v3, /device:TPU:0, one launch (start us, length us, event | category | flops | bytes accessed | tf_op | source)
XLA Modules:
  0.0 40.7 jit_solution(7859094610446222065)
XLA Ops:
  0.0 0.0 copy-start
  0.0 0.0 copy-start.1
  0.0 17.0 %gather.1 = (bf16[1155,8,256]{2,1,0:T(8,128)(2,1)S(1)}, bf16[1152,8,256]{2,1,0:T(8,128)(2,1)S(1)}, s32[3,16,256]{2,1,0:T(8,128)S(1)}, f32[784,256]{1,0:T(8,128)S...) custom-call(bf16[256,6272]{1,0:T(8,128)(2,1)} %nodes_ref.1, ...), custom_call_target="tpu_custom_call" | custom-call | tf_op jit(solution)/shard_map/gather/pallas_call | solution.py:481
  17.0 0.0 copy-done
  17.0 0.0 copy-done.1
  17.0 23.7 %layer.1 = bf16[256,6272]{1,0:T(8,128)(2,1)} custom-call(bf16[1155,8,256]{2,1,0:T(8,128)(2,1)S(1)} %get-tuple-element.12.table_ref, bf16[1152,8,256]{2,1,0:T(8,128)(2,1)S(1)} %get-tuple-element.13.gates_ref, s32[3,16,256]{2,1,0:T(8,128)S(1)} %get-tuple-element.14.rows_ref, f32[784,256]{1,0:T(8,128)S(1)} %get-tuple-element.15.harm_rows_ref, ...), custom_call_target="tpu_custom_call" | custom-call | tf_op jit(solution)/shard_map/layer/pallas_call | solution.py:530
Async XLA Ops:
  0.0 17.0 %copy-start = (bf16[256,6272]{1,0:T(8,128)(2,1)S(1)}, bf16[256,6272]{1,0:T(8,128)(2,1)}, u32[]{:S(2)}) copy-start(bf16[256,6272]{1,0:T(8,128)(2,1)} %nodes_ref.1) | copy-start | bytes 9633796
  0.0 17.0 %copy-start.1 = (f32[7,128]{1,0:T(8,128)S(1)}, f32[7,128]{1,0:T(8,128)}, u32[]{:S(2)}) copy-start(f32[7,128]{1,0:T(8,128)} %gain_ref.1) | copy-start | bytes 10756

commit v4 on v3

--- a/solution.py
+++ b/solution.py
@@ -27,11 +27,15 @@
 GE = GROUP * EB
 GN = GROUP * TB
 LENGTHS = 384
-ROWS = 48
+ROWS = 49
 CHUNK = 4
-CHUNKS = EB // CHUNK + 1
-SLOTS = CHUNK * CHUNKS
-ZERO_ROW = TABLE
+CHUNKS = BLOCKS * (EB // CHUNK + 1)
+WORK = 16
+QUARTERS = WORK // CHUNK
+STEPS = CHUNKS // QUARTERS
+LANES = 384
+LISTS = 2 * WORK + QUARTERS + 1
+FIXED = 8
 
 cutoff_radius = 6.0
 norm_eps = 1e-06
@@ -43,7 +47,6 @@
 DEGREE_OF = np.repeat(np.arange(LMAX + 1), 2 * np.arange(LMAX + 1) + 1)
 PARTS = 3
 WIDE = 2 * C
-LISTS = 80
 STEP = 8
 BAND = 32
 PIECE = 7 * C
@@ -140,7 +143,9 @@
     return jnp.sum(jnp.where(diagonal, jnp.broadcast_to(row, (size, size)), 0), axis=1, keepdims=True)
 
 
-def fill_lists(peer_ref, source_ref, target_ref, length_ref, peers, across_refs, slot_ref):
+def fill_lists(
+    peer_ref, source_ref, target_ref, length_ref, peers, across_refs, place_ref, list_ref, slot_ref
+):
     peer = jnp.concatenate([jnp.zeros((1, KEEP), I32), peer_ref[...]], axis=1)
     target = jnp.where(peer < peers, target_ref[...], TB)
     source = source_ref[...]
@@ -154,18 +159,79 @@
     one = (target == 1).astype(F32)
     rank0 = jnp.dot(lower, zero, preferred_element_type=F32).astype(I32)
     rank1 = jnp.dot(lower, one, preferred_element_type=F32).astype(I32)
-    slot = jnp.where(target == 0, rank0, jnp.where(target == 1, SLOTS - 1 - rank1, -1))
-    relative = (source - ZERO_ROW) * PARTS
-    length = length * PARTS
-    count0 = jnp.sum(zero, axis=0, keepdims=True).astype(I32)
-    rows = []
-    for s in range(SLOTS):
-        rows.append(jnp.sum(jnp.where(slot == s, relative, 0), axis=0, keepdims=True) + ZERO_ROW * PARTS)
-    rows.append(lax.shift_right_logical(count0 + (CHUNK - 1), 2))
-    for s in range(SLOTS):
-        rows.append(jnp.sum(jnp.where(slot == s, length, 0), axis=0, keepdims=True))
-    rows.append(jnp.zeros((LISTS - 2 * SLOTS - 1, BLOCKS), I32))
-    slot_ref[...] = jnp.concatenate(rows, axis=0)
+
+    def chunks(mask):
+        count = jnp.sum(mask, axis=0, keepdims=True).astype(I32)
+        return jnp.maximum(lax.shift_right_logical(count + (CHUNK - 1), 2), 1)
+
+    chunks0, chunks1 = chunks(zero), chunks(one)
+    before = (
+        lax.broadcasted_iota(I32, (BLOCKS, BLOCKS), 0) < lax.broadcasted_iota(I32, (BLOCKS, BLOCKS), 1)
+    ).astype(F32)
+    each = jnp.broadcast_to((chunks0 + chunks1).astype(F32), (8, BLOCKS))
+    start = jnp.dot(each, before, preferred_element_type=F32).astype(I32)
+    start0 = start[:1]
+    start1 = start0 + chunks0
+    place = jnp.where(target == 0, start0 * CHUNK + rank0, start1 * CHUNK + rank1)
+    place = jnp.where(target < TB, place, -1)
+    source = source + 1
+    for n, value in enumerate(
+        (
+            lax.bitwise_and(place, WORK - 1),
+            lax.shift_right_arithmetic(place, 4),
+            lax.shift_right_logical(source, 8),
+            lax.bitwise_and(source, 255),
+            lax.shift_right_logical(length, 8),
+            lax.bitwise_and(length, 255),
+        )
+    ):
+        place_ref[n] = value
+    list_ref[...] = jnp.zeros((4 * WORK, LANES), F32)
+
+    @pl.loop(0, EB // 4)
+    def _(step):
+        column = lax.broadcasted_iota(I32, (LANES, BLOCKS), 0)
+        lane = lax.broadcasted_iota(I32, (WORK, BLOCKS), 0)
+        total = None
+        for half in range(2):
+            lefts, rights = [], []
+            for n in range(2):
+                e = step * 4 + half * 2 + n
+                row = [place_ref[m, pl.ds(e, 1), :] for m in range(6)]
+                mine = lane == row[0]
+                lefts.append(
+                    jnp.concatenate([jnp.where(mine, row[m], 0) for m in range(2, 6)], axis=0)
+                    .astype(F32)
+                    .astype(BF16)
+                )
+                rights.append((column == row[1]).astype(F32).astype(BF16))
+            product = lax.dot_general(
+                jnp.concatenate(lefts, axis=1),
+                jnp.concatenate(rights, axis=1),
+                (((1,), (1,)), ((), ())),
+                preferred_element_type=F32,
+            )
+            total = product if total is None else total + product
+        list_ref[...] += total
+
+    found = list_ref[...].astype(I32)
+    slot_ref[:WORK, :] = (found[:WORK] * 256 + found[WORK : 2 * WORK]) * PARTS
+    slot_ref[WORK : 2 * WORK, :] = (found[2 * WORK : 3 * WORK] * 256 + found[3 * WORK :]) * PARTS
+    starts = jnp.concatenate([start0, start1, jnp.zeros((6, BLOCKS), I32)], axis=0).T
+    count = (start1 + chunks1)[:, BLOCKS - 1 :]
+    for q in range(QUARTERS):
+        chunk = lax.broadcasted_iota(I32, (BLOCKS, LANES), 1) * QUARTERS + q
+        reached = jnp.zeros((1, LANES), I32)
+        opened = jnp.zeros((1, LANES), I32)
+        for t in range(TB):
+            column = starts[:, t : t + 1]
+            reached = reached + jnp.sum((column <= chunk).astype(I32), axis=0, keepdims=True)
+            opened = opened + jnp.sum((column == chunk).astype(I32), axis=0, keepdims=True)
+        node = jnp.where(chunk[:1] < count, reached - 1, NODES)
+        slot_ref[2 * WORK + q : 2 * WORK + q + 1, :] = node * (2 * ROWS) + opened
+    slot_ref[LISTS - 1 : LISTS, :] = jnp.broadcast_to(
+        lax.shift_right_logical(count + (2 * QUARTERS - 1), 3), (1, LANES)
+    )
 
 
 def by_group(ref):
@@ -259,6 +325,8 @@
     length_across_ref,
     target_across_ref,
     turned_ref,
+    place_ref,
+    list_ref,
     load_sem,
     other_sem,
     send_sem,
@@ -327,12 +395,22 @@
     for load in smalls[1:5]:
         load.wait()
     across_refs = (source_across_ref, length_across_ref, target_across_ref)
-    fill_lists(peer_ref, source_ref, target_ref, length_ref, peers, across_refs, slot_ref)
+    fill_lists(
+        peer_ref,
+        source_ref,
+        target_ref,
+        length_ref,
+        peers,
+        across_refs,
+        place_ref,
+        list_ref,
+        slot_ref,
+    )
     smalls[5].wait()
     smalls[6].wait()
     fill_gates(radial_in_ref, radial_out_ref, gate_ref, gate0_ref, gates_ref)
-    spread_rows(nodes_ref, NODES, 0, wide_ref, table_ref)
-    table_ref[ZERO_ROW * PARTS :] = jnp.zeros((PARTS, 8, WIDE), BF16)
+    spread_rows(nodes_ref, NODES, 1, wide_ref, table_ref)
+    table_ref[:PARTS] = jnp.zeros((PARTS, 8, WIDE), BF16)
     smalls[7].wait()
     turn_harmonics(
         across_refs, harm_ref, scalars_ref, gate0_ref, turned_ref, rows_ref, harm_rows_ref, zeroth_ref
@@ -344,7 +422,7 @@
         weight_ref[degree] = jnp.dot(both, update_ref[degree], preferred_element_type=F32).astype(BF16)
     for copy in copies:
         copy.wait_recv()
-    spread_rows(arrived_ref, 4 * HALO, NODES, wide_ref, table_ref)
+    spread_rows(arrived_ref, 4 * HALO, NODES + 1, wide_ref, table_ref)
     scalars_ref[:NODES, :] = nodes_ref[:, :C]
     scalars_ref[NODES:, :] = arrived_ref[:, :C]
     zeroth_ref[0] = transposed(scalars_ref[...]).astype(BF16)
@@ -352,25 +430,21 @@
         copy.wait_send()
 
 
-def sum_edges(b, slots, table_ref, gates_ref, sums_ref):
-    first = slots[SLOTS][b]
-    total0 = jnp.zeros((PARTS, 8, WIDE), F32)
-    running = jnp.zeros((PARTS, 8, WIDE), F32)
-    for j in range(CHUNKS):
+def sum_edges(step, total, slots, table_ref, gates_ref, sums_ref):
+    for q in range(QUARTERS):
         parts = []
-        for k in range(CHUNK):
-            at = j * CHUNK + k
+        for k in range(q * CHUNK, (q + 1) * CHUNK):
             parts.append(
-                table_ref[pl.ds(slots[at][b], PARTS)] * gates_ref[pl.ds(slots[SLOTS + 1 + at][b], PARTS)]
+                table_ref[pl.ds(slots[k][step], PARTS)] * gates_ref[pl.ds(slots[WORK + k][step], PARTS)]
             )
         part = ((parts[0] + parts[1]) + (parts[2] + parts[3])).astype(F32)
-        running = running + part
-        total0 = jnp.where(j < first, running, total0)
-    at = pl.multiple_of(b * (2 * ROWS), 8)
-    for t, total in enumerate((total0, running - total0)):
+        word = slots[2 * WORK + q][step]
+        total = jnp.where(lax.bitwise_and(word, 1) == 1, part, total + part)
+        at = lax.shift_right_logical(word, 1)
         for tile in range(6):
             i, h = divmod(tile, 2)
-            sums_ref[pl.ds(at + t * ROWS + 8 * tile, 8), :] = total[i, :, h * C : (h + 1) * C]
+            sums_ref[pl.ds(at + 8 * tile, 8), :] = total[i, :, h * C : (h + 1) * C]
+    return total
 
 
 def sum_blocks(slots, rows_ref, harm_rows_ref, zeroth_ref, table_ref, gates_ref, sums_ref, harm_sums_ref, first_ref):
@@ -379,11 +453,19 @@
     same_block = lax.shift_right_logical(node, 1) == lax.shift_right_logical(edge, 5)
     wanted = jnp.where(same_block, lax.bitwise_and(node, 1), -1)
 
-    @pl.loop(0, GROUPS)
-    def _(g):
+    def both(g, total):
         harmonic_sums(g, wanted, rows_ref, harm_rows_ref, zeroth_ref, harm_sums_ref, first_ref)
-        for n in range(GROUP):
-            sum_edges(g * GROUP + n, slots, table_ref, gates_ref, sums_ref)
+        for n in range(FIXED):
+            total = sum_edges(g * FIXED + n, total, slots, table_ref, gates_ref, sums_ref)
+        return total
+
+    def rest(pair, total):
+        for n in range(2):
+            total = sum_edges(pair * 2 + n, total, slots, table_ref, gates_ref, sums_ref)
+        return total
+
+    total = lax.fori_loop(0, GROUPS, both, jnp.zeros((PARTS, 8, WIDE), F32))
+    lax.fori_loop(GROUPS * FIXED // 2, slots[LISTS - 1][0], rest, total)
 
 
 def update_nodes(nodes_ref, sums_ref, first_ref, harm_sums_ref, weight_ref, squares_ref, combined_ref):
@@ -486,7 +568,7 @@
             pltpu.VMEM((3, GROUPS, GE), I32),
             pltpu.VMEM((COEF * GROUPS, GE), F32),
             pltpu.VMEM((2, C, TABLE), BF16),
-            pltpu.VMEM((LISTS, BLOCKS), I32),
+            pltpu.VMEM((40, LANES), I32),
             pltpu.VMEM((DEG, 2 * C, C), BF16),
         ),
         in_specs=[HBM] * 12,
@@ -514,6 +596,8 @@
             pltpu.VMEM((BLOCKS, EB), I32),
             pltpu.VMEM((BLOCKS, EB), I32),
             pltpu.VMEM((7, BLOCKS, EB), F32),
+            pltpu.VMEM((6, EB, BLOCKS), I32),
+            pltpu.VMEM((4 * WORK, LANES), F32),
             pltpu.SemaphoreType.DMA((PIECES,)),
             pltpu.SemaphoreType.DMA((11,)),
             pltpu.SemaphoreType.DMA((4, PIECES)),
@@ -533,16 +617,16 @@
         in_specs=[VMEM] * len(arrays),
         out_specs=ANY,
         scratch_shapes=[
-            pltpu.VMEM((NODES * ROWS, C), F32),
+            pltpu.VMEM(((NODES + 1) * ROWS, C), F32),
             pltpu.VMEM((COEF, NODES, C), F32),
             pltpu.VMEM((NODES, C), F32),
             pltpu.VMEM((NODES, C), F32),
             pltpu.VMEM((NODES, FEAT), F32),
             pltpu.VMEM((NODES, FEAT), BF16),
-            pltpu.SemaphoreType.DMA((2 * SLOTS + 1,)),
+            pltpu.SemaphoreType.DMA((LISTS,)),
             pltpu.SemaphoreType.DMA((NODES // BAND,)),
         ]
-        + [pltpu.SMEM((BLOCKS,), I32)] * (2 * SLOTS + 1),
+        + [pltpu.SMEM((LANES,), I32)] * LISTS,
         compiler_params=pltpu.CompilerParams(vmem_limit_bytes=LAYER_VMEM),
         name="layer",
     )(*arrays)

time: 40.8 us -> 36.8 us (0.902)
  Pallas kernels: 40.7 us -> 36.7 us
    pallas_call x1, Pallas kernels: 23.7 us -> 19.5 us  [layer(): pl.pallas_call(layer_kernel, out_shape=jax.ShapeDtypeStruct((NODES, FEAT)...]
where the time goes in v4:
time: 36.8 us; the launch traced here: 36.7 us
  Pallas kernels  36.7 us (100%)
    pallas_call x1, Pallas kernels, layer(): pl.pallas_call(layer_kernel, out_shape=jax.ShapeDtypeStruct((NODES, FEAT)...  19.5 us
    pallas_call x1, Pallas kernels, gather(): pl.pallas_call(functools.partial(gather_kernel, peers=peers, columns=colu...  17.2 us

profile of v4, /device:TPU:0, one launch (start us, length us, event | category | flops | bytes accessed | tf_op | source)
XLA Modules:
  0.0 36.7 jit_solution(4423539063583449644)
XLA Ops:
  0.0 0.0 copy-start
  0.0 0.0 copy-start.1
  0.0 17.2 %gather.1 = (bf16[1155,8,256]{2,1,0:T(8,128)(2,1)S(1)}, bf16[1152,8,256]{2,1,0:T(8,128)(2,1)S(1)}, s32[3,16,256]{2,1,0:T(8,128)S(1)}, f32[784,256]{1,0:T(8,128)S...) custom-call(bf16[256,6272]{1,0:T(8,128)(2,1)} %nodes_ref.1, ...), custom_call_target="tpu_custom_call" | custom-call | tf_op jit(solution)/shard_map/gather/pallas_call | solution.py:563
  17.2 0.0 copy-done
  17.2 0.0 copy-done.1
  17.2 19.5 %layer.1 = bf16[256,6272]{1,0:T(8,128)(2,1)} custom-call(bf16[1155,8,256]{2,1,0:T(8,128)(2,1)S(1)} %get-tuple-element.12.table_ref, bf16[1152,8,256]{2,1,0:T(8,128)(2,1)S(1)} %get-tuple-element.13.gates_ref, s32[3,16,256]{2,1,0:T(8,128)S(1)} %get-tuple-element.14.rows_ref, f32[784,256]{1,0:T(8,128)S(1)} %get-tuple-element.15.harm_rows_ref, ...), custom_call_target="tpu_custom_call" | custom-call | tf_op jit(solution)/shard_map/layer/pallas_call | solution.py:614
Async XLA Ops:
  0.0 17.2 %copy-start = (bf16[256,6272]{1,0:T(8,128)(2,1)S(1)}, bf16[256,6272]{1,0:T(8,128)(2,1)}, u32[]{:S(2)}) copy-start(bf16[256,6272]{1,0:T(8,128)(2,1)} %nodes_ref.1) | copy-start | bytes 9633796
  0.0 17.2 %copy-start.1 = (f32[7,128]{1,0:T(8,128)S(1)}, f32[7,128]{1,0:T(8,128)}, u32[]{:S(2)}) copy-start(f32[7,128]{1,0:T(8,128)} %gain_ref.1) | copy-start | bytes 10756

commit v5 on v4

--- a/solution.py
+++ b/solution.py
@@ -35,7 +35,7 @@
 STEPS = CHUNKS // QUARTERS
 LANES = 384
 LISTS = 2 * WORK + QUARTERS + 1
-FIXED = 8
+FIXED = 12
 
 cutoff_radius = 6.0
 norm_eps = 1e-06
@@ -47,7 +47,7 @@
 DEGREE_OF = np.repeat(np.arange(LMAX + 1), 2 * np.arange(LMAX + 1) + 1)
 PARTS = 3
 WIDE = 2 * C
-STEP = 8
+STEP = 16
 BAND = 32
 PIECE = 7 * C
 PIECES = FEAT // PIECE
@@ -80,7 +80,7 @@
     )
 
 
-def fill_gates(radial_in_ref, radial_out_ref, gate_ref, gate0_ref, table_ref):
+def fill_basis(basis_ref):
     i = lax.broadcasted_iota(I32, (LENGTHS, RB), 0).astype(F32)
     r = length_of(i)
     k = lax.broadcasted_iota(I32, (LENGTHS, RB), 1).astype(F32)
@@ -89,11 +89,15 @@
     along = length_of(lax.broadcasted_iota(I32, (8, LENGTHS), 1).astype(F32))
     envelope = (0.5 * (jnp.cos(jnp.pi * along / cutoff_radius) + 1.0)).T[:, :1]
     offsets = (r - centers) / spread
-    basis = (jnp.exp(-0.5 * offsets * offsets) * envelope).astype(BF16)
+    basis_ref[...] = (jnp.exp(-0.5 * offsets * offsets) * envelope).astype(BF16)
+
+
+def fill_gates(basis_ref, radial_in_ref, radial_out_ref, gate_ref, gate0_ref, table_ref):
     hidden = lax.dot_general(
-        basis, radial_in_ref[...], (((1,), (1,)), ((), ())), preferred_element_type=F32
-    )
-    hidden = jax.nn.silu(hidden).astype(BF16)
+        basis_ref[...], radial_in_ref[...], (((1,), (1,)), ((), ())), preferred_element_type=F32
+    )
+    half = 0.5 * hidden
+    hidden = (half * jnp.tanh(half) + half).astype(BF16)
     gate = jnp.dot(hidden, radial_out_ref[...], preferred_element_type=F32).astype(BF16)
     gate0_ref[...] = gate[:, :C]
     gate_ref[...] = gate.astype(F32)
@@ -121,12 +125,12 @@
                 ).astype(BF16)
 
 
-def spread_rows(source_ref, count, base, wide_ref, table_ref):
+def spread_rows(source_ref, count, first, base, wide_ref, table_ref):
     @pl.loop(0, count // 16)
     def _(g):
         at = pl.multiple_of(g * 16, 16)
         for lm in range(1, COEF, 2):
-            pair = source_ref[pl.ds(at, 16), lm * C : (lm + 2) * C].astype(F32)
+            pair = source_ref[pl.ds(pl.multiple_of(first + at, 16), 16), lm * C : (lm + 2) * C].astype(F32)
             wide_ref[pl.ds(lm - 1, 16, stride=ROWS), :] = pair[:, :C]
             wide_ref[pl.ds(lm, 16, stride=ROWS), :] = pair[:, C:]
         to = (base + at) * PARTS
@@ -246,9 +250,7 @@
     return lax.dot_general(identity, x, (((1,), (1,)), ((), ())), preferred_element_type=F32)
 
 
-def turn_harmonics(
-    across_refs, harm_ref, scalars_ref, gate0_ref, turned_ref, rows_ref, harm_rows_ref, zeroth_ref
-):
+def turn_harmonics(across_refs, harm_ref, turned_ref, rows_ref, harm_rows_ref):
     for n, ref in enumerate(across_refs):
         rows_ref[n] = by_group(ref)
 
@@ -256,10 +258,7 @@
     def _(step):
         for n in range(7):
             turned_ref[n] = harm_ref[step * 7 + n].astype(F32).T
-            at = pl.multiple_of((step * 7 + n) * GROUPS, GROUPS)
-            harm_rows_ref[pl.ds(at, GROUPS), :] = by_group(turned_ref.at[n])
-
-    zeroth_ref[1] = transposed(gate0_ref[...]).astype(BF16)
+            harm_rows_ref[step * 7 + n] = by_group(turned_ref.at[n])
 
 
 def harmonic_sums(g, wanted, rows_ref, harm_rows_ref, zeroth_ref, harm_sums_ref, first_ref):
@@ -275,7 +274,7 @@
         mask.astype(BF16), scalar * gate, across, preferred_element_type=F32
     )
     left = jnp.concatenate(
-        [(harm_rows_ref[pl.ds(lm * GROUPS + g, 1), :] * mask).astype(BF16) for lm in range(COEF)],
+        [(harm_rows_ref[lm, pl.ds(g, 1), :] * mask).astype(BF16) for lm in range(COEF)],
         axis=0,
     )
     right = lax.dot_general(left, scalar, across, preferred_element_type=F32)
@@ -300,7 +299,8 @@
     gates_ref,
     rows_ref,
     harm_rows_ref,
-    zeroth_ref,
+    gate_turned_ref,
+    scalars_ref,
     slot_ref,
     weight_ref,
     halo_ref,
@@ -320,13 +320,13 @@
     gate_ref,
     gate0_ref,
     wide_ref,
-    scalars_ref,
     source_across_ref,
     length_across_ref,
     target_across_ref,
     turned_ref,
     place_ref,
     list_ref,
+    basis_ref,
     load_sem,
     other_sem,
     send_sem,
@@ -370,6 +370,7 @@
     for neighbour in neighbours:
         pl.semaphore_signal(barrier, inc=1, device_id=neighbour, device_id_type=MESH)
 
+    fill_basis(basis_ref)
     smalls[0].wait()
     index = column_of(jnp.concatenate([halo_ref[k : k + 1, :] for k in range(4)], axis=1), 4 * HALO)
     pick = (lax.broadcasted_iota(I32, (4 * HALO, NODES), 1) == index).astype(F32).astype(BF16)
@@ -408,24 +409,26 @@
     )
     smalls[5].wait()
     smalls[6].wait()
-    fill_gates(radial_in_ref, radial_out_ref, gate_ref, gate0_ref, gates_ref)
-    spread_rows(nodes_ref, NODES, 1, wide_ref, table_ref)
+    fill_gates(basis_ref, radial_in_ref, radial_out_ref, gate_ref, gate0_ref, gates_ref)
+    spread_rows(nodes_ref, NODES, 0, 1, wide_ref, table_ref)
     table_ref[:PARTS] = jnp.zeros((PARTS, 8, WIDE), BF16)
     smalls[7].wait()
     turn_harmonics(
-        across_refs, harm_ref, scalars_ref, gate0_ref, turned_ref, rows_ref, harm_rows_ref, zeroth_ref
-    )
+        across_refs, harm_ref, turned_ref, rows_ref, harm_rows_ref
+    )
+    gate_turned_ref[...] = transposed(gate0_ref[...]).astype(BF16)
     for load in smalls[8:]:
         load.wait()
     for degree in range(DEG):
         both = jnp.concatenate([mix_ref[degree], harmonic_ref[...]], axis=0)
         weight_ref[degree] = jnp.dot(both, update_ref[degree], preferred_element_type=F32).astype(BF16)
-    for copy in copies:
-        copy.wait_recv()
-    spread_rows(arrived_ref, 4 * HALO, NODES + 1, wide_ref, table_ref)
     scalars_ref[:NODES, :] = nodes_ref[:, :C]
+    for n, first in enumerate((2, 0)):
+        for c in range(PIECES):
+            for copy in copies[4 * c + first : 4 * c + first + 2]:
+                copy.wait_recv()
+        spread_rows(arrived_ref, 2 * HALO, 2 * HALO * n, NODES + 1 + 2 * HALO * n, wide_ref, table_ref)
     scalars_ref[NODES:, :] = arrived_ref[:, :C]
-    zeroth_ref[0] = transposed(scalars_ref[...]).astype(BF16)
     for copy in copies:
         copy.wait_send()
 
@@ -439,7 +442,8 @@
             )
         part = ((parts[0] + parts[1]) + (parts[2] + parts[3])).astype(F32)
         word = slots[2 * WORK + q][step]
-        total = jnp.where(lax.bitwise_and(word, 1) == 1, part, total + part)
+        opens = lax.bitwise_and(jnp.full((1, 8, WIDE), word, I32), 1) == 1
+        total = jnp.where(opens, part, total + part)
         at = lax.shift_right_logical(word, 1)
         for tile in range(6):
             i, h = divmod(tile, 2)
@@ -454,9 +458,10 @@
     wanted = jnp.where(same_block, lax.bitwise_and(node, 1), -1)
 
     def both(g, total):
-        harmonic_sums(g, wanted, rows_ref, harm_rows_ref, zeroth_ref, harm_sums_ref, first_ref)
-        for n in range(FIXED):
-            total = sum_edges(g * FIXED + n, total, slots, table_ref, gates_ref, sums_ref)
+        for n in range(2):
+            harmonic_sums(2 * g + n, wanted, rows_ref, harm_rows_ref, zeroth_ref, harm_sums_ref, first_ref)
+        for n in range(2 * FIXED):
+            total = sum_edges(g * 2 * FIXED + n, total, slots, table_ref, gates_ref, sums_ref)
         return total
 
     def rest(pair, total):
@@ -464,7 +469,7 @@
             total = sum_edges(pair * 2 + n, total, slots, table_ref, gates_ref, sums_ref)
         return total
 
-    total = lax.fori_loop(0, GROUPS, both, jnp.zeros((PARTS, 8, WIDE), F32))
+    total = lax.fori_loop(0, GROUPS // 2, both, jnp.zeros((PARTS, 8, WIDE), F32))
     lax.fori_loop(GROUPS * FIXED // 2, slots[LISTS - 1][0], rest, total)
 
 
@@ -524,12 +529,14 @@
     gates_ref,
     rows_ref,
     harm_rows_ref,
-    zeroth_ref,
+    gate_turned_ref,
+    scalars_ref,
     slot_ref,
     weight_ref,
     gain_ref,
     nodes_ref,
     out_hbm,
+    zeroth_ref,
     sums_ref,
     harm_sums_ref,
     first_ref,
@@ -545,6 +552,8 @@
         copy = pltpu.make_async_copy(slot_ref.at[n], slot, slot_sem.at[n])
         copy.start()
         slot_copies.append(copy)
+    zeroth_ref[0] = transposed(scalars_ref[...]).astype(BF16)
+    zeroth_ref[1] = gate_turned_ref[...]
     for copy in slot_copies:
         copy.wait()
     sum_blocks(
@@ -566,13 +575,14 @@
             pltpu.VMEM(((TABLE + 1) * PARTS, 8, WIDE), BF16),
             pltpu.VMEM((LENGTHS * PARTS, 8, WIDE), BF16),
             pltpu.VMEM((3, GROUPS, GE), I32),
-            pltpu.VMEM((COEF * GROUPS, GE), F32),
-            pltpu.VMEM((2, C, TABLE), BF16),
+            pltpu.VMEM((COEF, GROUPS, GE), F32),
+            pltpu.VMEM((C, LENGTHS), BF16),
+            pltpu.VMEM((TABLE, C), BF16),
             pltpu.VMEM((40, LANES), I32),
             pltpu.VMEM((DEG, 2 * C, C), BF16),
         ),
         in_specs=[HBM] * 12,
-        out_specs=(VMEM,) * 7,
+        out_specs=(VMEM,) * 8,
         scratch_shapes=[
             pltpu.VMEM((4, HALO), I32),
             pltpu.VMEM((1, BLOCKS - KEEP), I32),
@@ -591,13 +601,13 @@
             pltpu.VMEM((LENGTHS, DEG * C), F32),
             pltpu.VMEM((LENGTHS, C), BF16),
             pltpu.VMEM((16 * ROWS, C), F32),
-            pltpu.VMEM((TABLE, C), BF16),
             pltpu.VMEM((BLOCKS, EB), I32),
             pltpu.VMEM((BLOCKS, EB), I32),
             pltpu.VMEM((BLOCKS, EB), I32),
             pltpu.VMEM((7, BLOCKS, EB), F32),
             pltpu.VMEM((6, EB, BLOCKS), I32),
             pltpu.VMEM((4 * WORK, LANES), F32),
+            pltpu.VMEM((LENGTHS, RB), BF16),
             pltpu.SemaphoreType.DMA((PIECES,)),
             pltpu.SemaphoreType.DMA((11,)),
             pltpu.SemaphoreType.DMA((4, PIECES)),
@@ -617,6 +627,7 @@
         in_specs=[VMEM] * len(arrays),
         out_specs=ANY,
         scratch_shapes=[
+            pltpu.VMEM((2, C, TABLE), BF16),
             pltpu.VMEM(((NODES + 1) * ROWS, C), F32),
             pltpu.VMEM((COEF, NODES, C), F32),
             pltpu.VMEM((NODES, C), F32),

time: 36.8 us -> 34.7 us (0.943)
  Pallas kernels: 36.7 us -> 34.6 us
    pallas_call x1, Pallas kernels: 19.5 us -> 17.8 us  [layer(): pl.pallas_call(layer_kernel, out_shape=jax.ShapeDtypeStruct((NODES, FEAT)...]
    pallas_call x1, Pallas kernels: 17.2 us -> 16.8 us  [gather(): pl.pallas_call(functools.partial(gather_kernel, peers=peers, columns=colu...]
where the time goes in v5:
time: 34.7 us; the launch traced here: 34.6 us
  Pallas kernels  34.6 us (100%)
    pallas_call x1, Pallas kernels, layer(): pl.pallas_call(layer_kernel, out_shape=jax.ShapeDtypeStruct((NODES, FEAT)...  17.8 us
    pallas_call x1, Pallas kernels, gather(): pl.pallas_call(functools.partial(gather_kernel, peers=peers, columns=colu...  16.8 us

profile of v5, /device:TPU:0, one launch (start us, length us, event | category | flops | bytes accessed | tf_op | source)
XLA Modules:
  0.0 34.6 jit_solution(13456241258726579316)
XLA Ops:
  0.0 0.0 copy-start
  0.0 0.0 copy-start.1
  0.0 16.8 %gather.1 = (bf16[1155,8,256]{2,1,0:T(8,128)(2,1)S(1)}, bf16[1152,8,256]{2,1,0:T(8,128)(2,1)S(1)}, s32[3,16,256]{2,1,0:T(8,128)S(1)}, f32[49,16,256]{2,1,0:T(8,1...) custom-call(bf16[256,6272]{1,0:T(8,128)(2,1)} %nodes_ref.1, ...), custom_call_target="tpu_custom_call" | custom-call | tf_op jit(solution)/shard_map/gather/pallas_call | solution.py:572
  16.8 0.0 copy-done
  16.8 0.0 copy-done.1
  16.8 17.8 %layer.1 = bf16[256,6272]{1,0:T(8,128)(2,1)} custom-call(bf16[1155,8,256]{2,1,0:T(8,128)(2,1)S(1)} %get-tuple-element.13.table_ref, bf16[1152,8,256]{2,1,0:T(8,128)(2,1)S(1)} %get-tuple-element.14.gates_ref, s32[3,16,256]{2,1,0:T(8,128)S(1)} %get-tuple-element.15.rows_ref, f32[49,16,256]{2,1,0:T(8,128)S(1)} %get-tuple-element.16.harm_rows_ref, ...), custom_call_target="tpu_custom_call" | custom-call | tf_op jit(solution)/shard_map/layer/pallas_call | solution.py:624
Async XLA Ops:
  0.0 16.8 %copy-start = (bf16[256,6272]{1,0:T(8,128)(2,1)S(1)}, bf16[256,6272]{1,0:T(8,128)(2,1)}, u32[]{:S(2)}) copy-start(bf16[256,6272]{1,0:T(8,128)(2,1)} %nodes_ref.1) | copy-start | bytes 9633796
  0.0 16.8 %copy-start.1 = (f32[7,128]{1,0:T(8,128)S(1)}, f32[7,128]{1,0:T(8,128)}, u32[]{:S(2)}) copy-start(f32[7,128]{1,0:T(8,128)} %gain_ref.1) | copy-start | bytes 10756

commit v6 on v5

--- a/solution.py
+++ b/solution.py
@@ -35,7 +35,7 @@
 STEPS = CHUNKS // QUARTERS
 LANES = 384
 LISTS = 2 * WORK + QUARTERS + 1
-FIXED = 12
+FIXED = 28
 
 cutoff_radius = 6.0
 norm_eps = 1e-06
@@ -49,8 +49,9 @@
 WIDE = 2 * C
 STEP = 16
 BAND = 32
-PIECE = 7 * C
-PIECES = FEAT // PIECE
+SIZES = (2, 4, 6, 9, 9, 9, 10)
+CUTS = tuple((C * sum(SIZES[:n]), C * size) for n, size in enumerate(SIZES))
+PIECES = len(CUTS)
 MESH = pl.DeviceIdType.MESH
 
 
@@ -190,11 +191,11 @@
         )
     ):
         place_ref[n] = value
-    list_ref[...] = jnp.zeros((4 * WORK, LANES), F32)
+    list_ref[...] = jnp.zeros((4 * WORK, STEPS), F32)
 
     @pl.loop(0, EB // 4)
     def _(step):
-        column = lax.broadcasted_iota(I32, (LANES, BLOCKS), 0)
+        column = lax.broadcasted_iota(I32, (STEPS, BLOCKS), 0)
         lane = lax.broadcasted_iota(I32, (WORK, BLOCKS), 0)
         total = None
         for half in range(2):
@@ -218,7 +219,9 @@
             total = product if total is None else total + product
         list_ref[...] += total
 
-    found = list_ref[...].astype(I32)
+    found = jnp.concatenate(
+        [list_ref[...].astype(I32), jnp.zeros((4 * WORK, LANES - STEPS), I32)], axis=1
+    )
     slot_ref[:WORK, :] = (found[:WORK] * 256 + found[WORK : 2 * WORK]) * PARTS
     slot_ref[WORK : 2 * WORK, :] = (found[2 * WORK : 3 * WORK] * 256 + found[3 * WORK :]) * PARTS
     starts = jnp.concatenate([start0, start1, jnp.zeros((6, BLOCKS), I32)], axis=0).T
@@ -359,7 +362,7 @@
     smalls[0].start()
     loads = []
     for c in range(PIECES):
-        cut = pl.ds(c * PIECE, PIECE)
+        cut = pl.ds(*CUTS[c])
         load = pltpu.make_async_copy(nodes_hbm.at[:, cut], nodes_ref.at[:, cut], load_sem.at[c])
         load.start()
         loads.append(load)
@@ -375,23 +378,28 @@
     index = column_of(jnp.concatenate([halo_ref[k : k + 1, :] for k in range(4)], axis=1), 4 * HALO)
     pick = (lax.broadcasted_iota(I32, (4 * HALO, NODES), 1) == index).astype(F32).astype(BF16)
     pl.semaphore_wait(barrier, 4)
-    copies = []
+
+    def send(k, c, cut):
+        part = pl.ds(k * HALO, HALO)
+        copy = pltpu.make_async_remote_copy(
+            src_ref=send_ref.at[part, cut],
+            dst_ref=arrived_ref.at[part, cut],
+            send_sem=send_sem.at[k, c],
+            recv_sem=recv_sem.at[k, c],
+            device_id=neighbours[k],
+            device_id_type=MESH,
+        )
+        copy.start()
+        return copy
+
+    above_below = []
     for c in range(PIECES):
         loads[c].wait()
-        cut = pl.ds(c * PIECE, PIECE)
+        cut = pl.ds(*CUTS[c])
         send_ref[:, cut] = jnp.dot(pick, nodes_ref[:, cut], preferred_element_type=F32).astype(BF16)
-        for k in (2, 3, 0, 1):
-            part = pl.ds(k * HALO, HALO)
-            copy = pltpu.make_async_remote_copy(
-                src_ref=send_ref.at[part, cut],
-                dst_ref=arrived_ref.at[part, cut],
-                send_sem=send_sem.at[k, c],
-                recv_sem=recv_sem.at[k, c],
-                device_id=neighbours[k],
-                device_id_type=MESH,
-            )
-            copy.start()
-            copies.append(copy)
+        for k in (2, 3):
+            above_below.append(send(k, c, cut))
+    ahead_behind = [send(k, 0, pl.ds(0, FEAT)) for k in (0, 1)]
 
     for load in smalls[1:5]:
         load.wait()
@@ -423,13 +431,12 @@
         both = jnp.concatenate([mix_ref[degree], harmonic_ref[...]], axis=0)
         weight_ref[degree] = jnp.dot(both, update_ref[degree], preferred_element_type=F32).astype(BF16)
     scalars_ref[:NODES, :] = nodes_ref[:, :C]
-    for n, first in enumerate((2, 0)):
-        for c in range(PIECES):
-            for copy in copies[4 * c + first : 4 * c + first + 2]:
-                copy.wait_recv()
+    for n, copies in enumerate((ahead_behind, above_below)):
+        for copy in copies:
+            copy.wait_recv()
         spread_rows(arrived_ref, 2 * HALO, 2 * HALO * n, NODES + 1 + 2 * HALO * n, wide_ref, table_ref)
     scalars_ref[NODES:, :] = arrived_ref[:, :C]
-    for copy in copies:
+    for copy in ahead_behind + above_below:
         copy.wait_send()
 
 
@@ -451,17 +458,22 @@
     return total
 
 
-def sum_blocks(slots, rows_ref, harm_rows_ref, zeroth_ref, table_ref, gates_ref, sums_ref, harm_sums_ref, first_ref):
+def sum_blocks(slot_copies, slots, rows_ref, harm_rows_ref, zeroth_ref, table_ref, gates_ref, sums_ref, harm_sums_ref, first_ref):
     node = lax.broadcasted_iota(I32, (GN, GE), 0)
     edge = lax.broadcasted_iota(I32, (GN, GE), 1)
     same_block = lax.shift_right_logical(node, 1) == lax.shift_right_logical(edge, 5)
     wanted = jnp.where(same_block, lax.bitwise_and(node, 1), -1)
 
+    for n in range(2):
+        harmonic_sums(n, wanted, rows_ref, harm_rows_ref, zeroth_ref, harm_sums_ref, first_ref)
+    for copy in slot_copies:
+        copy.wait()
+
     def both(g, total):
         for n in range(2):
-            harmonic_sums(2 * g + n, wanted, rows_ref, harm_rows_ref, zeroth_ref, harm_sums_ref, first_ref)
-        for n in range(2 * FIXED):
-            total = sum_edges(g * 2 * FIXED + n, total, slots, table_ref, gates_ref, sums_ref)
+            harmonic_sums(2 * g + 2 + n, wanted, rows_ref, harm_rows_ref, zeroth_ref, harm_sums_ref, first_ref)
+        for n in range(FIXED):
+            total = sum_edges(g * FIXED + n, total, slots, table_ref, gates_ref, sums_ref)
         return total
 
     def rest(pair, total):
@@ -469,8 +481,8 @@
             total = sum_edges(pair * 2 + n, total, slots, table_ref, gates_ref, sums_ref)
         return total
 
-    total = lax.fori_loop(0, GROUPS // 2, both, jnp.zeros((PARTS, 8, WIDE), F32))
-    lax.fori_loop(GROUPS * FIXED // 2, slots[LISTS - 1][0], rest, total)
+    total = lax.fori_loop(0, GROUPS // 2 - 1, both, jnp.zeros((PARTS, 8, WIDE), F32))
+    lax.fori_loop((GROUPS // 2 - 1) * FIXED // 2, slots[LISTS - 1][0], rest, total)
 
 
 def update_nodes(nodes_ref, sums_ref, first_ref, harm_sums_ref, weight_ref, squares_ref, combined_ref):
@@ -554,10 +566,8 @@
         slot_copies.append(copy)
     zeroth_ref[0] = transposed(scalars_ref[...]).astype(BF16)
     zeroth_ref[1] = gate_turned_ref[...]
-    for copy in slot_copies:
-        copy.wait()
     sum_blocks(
-        slots, rows_ref, harm_rows_ref, zeroth_ref, table_ref, gates_ref, sums_ref, harm_sums_ref, first_ref
+        slot_copies, slots, rows_ref, harm_rows_ref, zeroth_ref, table_ref, gates_ref, sums_ref, harm_sums_ref, first_ref
     )
     update_nodes(nodes_ref, sums_ref, first_ref, harm_sums_ref, weight_ref, squares_ref, combined_ref)
     store_nodes(squares_ref, gain_ref, combined_ref, out_ref, out_hbm, out_sem)
@@ -606,7 +616,7 @@
             pltpu.VMEM((BLOCKS, EB), I32),
             pltpu.VMEM((7, BLOCKS, EB), F32),
             pltpu.VMEM((6, EB, BLOCKS), I32),
-            pltpu.VMEM((4 * WORK, LANES), F32),
+            pltpu.VMEM((4 * WORK, STEPS), F32),
             pltpu.VMEM((LENGTHS, RB), BF16),
             pltpu.SemaphoreType.DMA((PIECES,)),
             pltpu.SemaphoreType.DMA((11,)),

time: 34.7 us -> 34.5 us (level)
    pallas_call x1, Pallas kernels: 17.8 us -> 17.4 us  [layer(): pl.pallas_call(layer_kernel, out_shape=jax.ShapeDtypeStruct((NODES, FEAT)...]
where the time goes in v6:
time: 34.5 us; the launch traced here: 34.4 us
  Pallas kernels  34.3 us (99%)
    pallas_call x1, Pallas kernels, layer(): pl.pallas_call(layer_kernel, out_shape=jax.ShapeDtypeStruct((NODES, FEAT)...  17.4 us
    pallas_call x1, Pallas kernels, gather(): pl.pallas_call(functools.partial(gather_kernel, peers=peers, columns=colu...  16.9 us

profile of v6, /device:TPU:0, one launch (start us, length us, event | category | flops | bytes accessed | tf_op | source)
XLA Modules:
  0.0 34.4 jit_solution(17501559471828578723)
XLA Ops:
  0.0 0.0 copy-start
  0.0 0.0 copy-start.1
  0.0 16.9 %gather.1 = (bf16[1155,8,256]{2,1,0:T(8,128)(2,1)S(1)}, bf16[1152,8,256]{2,1,0:T(8,128)(2,1)S(1)}, s32[3,16,256]{2,1,0:T(8,128)S(1)}, f32[49,16,256]{2,1,0:T(8,1...) custom-call(bf16[256,6272]{1,0:T(8,128)(2,1)} %nodes_ref.1, ...), custom_call_target="tpu_custom_call" | custom-call | tf_op jit(solution)/shard_map/gather/pallas_call | solution.py:582
  16.9 0.0 copy-done
  16.9 0.0 copy-done.1
  16.9 17.4 %layer.1 = bf16[256,6272]{1,0:T(8,128)(2,1)} custom-call(bf16[1155,8,256]{2,1,0:T(8,128)(2,1)S(1)} %get-tuple-element.13.table_ref, bf16[1152,8,256]{2,1,0:T(8,128)(2,1)S(1)} %get-tuple-element.14.gates_ref, s32[3,16,256]{2,1,0:T(8,128)S(1)} %get-tuple-element.15.rows_ref, f32[49,16,256]{2,1,0:T(8,128)S(1)} %get-tuple-element.16.harm_rows_ref, ...), custom_call_target="tpu_custom_call" | custom-call | tf_op jit(solution)/shard_map/layer/pallas_call | solution.py:634
Async XLA Ops:
  0.0 16.9 %copy-start = (bf16[256,6272]{1,0:T(8,128)(2,1)S(1)}, bf16[256,6272]{1,0:T(8,128)(2,1)}, u32[]{:S(2)}) copy-start(bf16[256,6272]{1,0:T(8,128)(2,1)} %nodes_ref.1) | copy-start | bytes 9633796
  0.0 16.9 %copy-start.1 = (f32[7,128]{1,0:T(8,128)S(1)}, f32[7,128]{1,0:T(8,128)}, u32[]{:S(2)}) copy-start(f32[7,128]{1,0:T(8,128)} %gain_ref.1) | copy-start | bytes 10756
